TPU v7x, 256 devices: a whole 4x4x8 slice. The times are simulated.
256 devices in a mesh: gx: 4 (over y), gy: 8 (over x, z_hi), gz: 8 (over z_lo, core).
Axes of the slice: x: 4, y: 4, z: 8 (z_hi: 2, z_lo: 4; z = z_hi * 4 + z_lo), core: 2. Of those that a mesh axis runs over, the one named last changes fastest.
Arguments:
- noisy: float32 [128, 128, 1024], P('gz', 'gx', 'gy'), may hold values from -6 to 6
Outputs:
- denoised: float32 [128, 128, 1024], P('gz', 'gx', 'gy')
All inputs are finite; a program needn't handle non-finite values.
Results may differ from a plain program's by a relative error of at most 0.0003.
Values sent between devices are 32-bit elements; how exact they have to be, the bound alone decides.
A program may use at most 64 MiB of HBM per device.

v0:
```python
import jax
import jax.numpy as jnp
from jax import lax
from jax.sharding import PartitionSpec as P

HALF_OFFSETS = [
    (step_z, step_x, step_y)
    for step_z in (-1, 0, 1)
    for step_x in (-1, 0, 1)
    for step_y in (-1, 0, 1)
    if (step_z, step_x, step_y) > (0, 0, 0)
]
INV_PATCH = 1.0 / 343.0


def extended_2(x, sides, width):
    for axis, dim in sides:
        size, length = (lax.axis_size(axis), x.shape[dim])
        up = [(i, (i + 1) % size) for i in range(size - 1)]
        down = [(j, i) for i, j in up]
        last = lax.slice_in_dim(x, length - width, length, axis=dim)
        leading = lax.slice_in_dim(x, 0, width, axis=dim)
        before = lax.ppermute(last, axis, up)
        after = lax.ppermute(leading, axis, down)
        x = jnp.concatenate([before, x, after], axis=dim)
    return x


def passed_along(x, axis, by):
    length = lax.axis_size(axis)
    pairs = [(i, i + by) for i in range(length) if 0 <= i + by < length]
    return lax.ppermute(x, axis, pairs)


def box_sum(field):
    length = field.shape[0] - 6
    total = field[0:length]
    for shift_by in range(1, 7):
        total = total + field[shift_by : shift_by + length]
    length = field.shape[1] - 6
    second = total[:, 0:length]
    for shift_by in range(1, 7):
        second = second + total[:, shift_by : shift_by + length]
    length = field.shape[2] - 6
    third = second[:, :, 0:length]
    for shift_by in range(1, 7):
        third = third + second[:, :, shift_by : shift_by + length]
    return third


def pair_weights(extended, start, extent, offset):
    low = start - 3
    base = extended[low : low + extent[0] + 6, low : low + extent[1] + 6, low : low + extent[2] + 6]
    moved = extended[
        low + offset[0] : low + offset[0] + extent[0] + 6,
        low + offset[1] : low + offset[1] + extent[1] + 6,
        low + offset[2] : low + offset[2] + extent[2] + 6,
    ]
    diff = base - moved
    return jnp.exp(-box_sum(diff * diff) * INV_PATCH)


def inside(start, length, total):
    coords = start + jnp.arange(length, dtype=jnp.int32)
    return ((coords >= 0) & (coords < total)).astype(jnp.float32)


def region_mask(margin, shape):
    size_z, size_x, size_y = shape
    mask_z = inside(
        lax.axis_index("gz") * size_z - margin, size_z + 2 * margin, size_z * lax.axis_size("gz")
    )
    mask_x = inside(
        lax.axis_index("gx") * size_x - margin, size_x + 2 * margin, size_x * lax.axis_size("gx")
    )
    mask_y = inside(
        lax.axis_index("gy") * size_y - margin, size_y + 2 * margin, size_y * lax.axis_size("gy")
    )
    return mask_z[:, None, None] * mask_x[None, :, None] * mask_y[None, None, :]


def fold_rim(volume, along):
    length = volume.shape[along]
    core = lax.slice_in_dim(volume, 2, length - 2, axis=along)
    lowest = lax.slice_in_dim(volume, 0, 1, axis=along)
    highest = lax.slice_in_dim(volume, length - 1, length, axis=along)
    widths_low = [(0, 0)] * volume.ndim
    widths_high = [(0, 0)] * volume.ndim
    widths_low[along] = (0, length - 5)
    widths_high[along] = (length - 5, 0)
    return core + jnp.pad(lowest, widths_low) + jnp.pad(highest, widths_high)


def place_shifted(values, offset):
    return jnp.pad(
        values,
        (
            (1 + offset[0], 1 - offset[0]),
            (1 + offset[1], 1 - offset[1]),
            (1 + offset[2], 1 - offset[2]),
        ),
    )


def shards(noisy):
    size_z, size_x, size_y = noisy.shape
    extended = extended_2(noisy, (("gx", 1), ("gy", 2), ("gz", 0)), 4)
    region = region_mask(1, noisy.shape)
    central_num = jnp.zeros(noisy.shape, jnp.float32)
    central_w = jnp.zeros(noisy.shape, jnp.float32)
    credit_num = jnp.zeros((size_z + 2, size_x + 2, size_y + 2), jnp.float32)
    credit_w = jnp.zeros((size_z + 2, size_x + 2, size_y + 2), jnp.float32)
    for offset in HALF_OFFSETS:
        weights = pair_weights(extended, 4, noisy.shape, offset)
        weights = (
            weights
            * region[
                1 + offset[0] : 1 + offset[0] + size_z,
                1 + offset[1] : 1 + offset[1] + size_x,
                1 + offset[2] : 1 + offset[2] + size_y,
            ]
        )
        partner = extended[
            4 + offset[0] : 4 + offset[0] + size_z,
            4 + offset[1] : 4 + offset[1] + size_x,
            4 + offset[2] : 4 + offset[2] + size_y,
        ]
        central_num = central_num + weights * partner
        central_w = central_w + weights
        credit_num = credit_num + place_shifted(weights * noisy, offset)
        credit_w = credit_w + place_shifted(weights, offset)
    numerator = credit_num + jnp.pad(central_num, 1)
    weight_sum = credit_w + jnp.pad(central_w, 1)
    stacked = jnp.stack([numerator, weight_sum])
    upper_layer = stacked[:, size_z + 1 : size_z + 2]
    from_below = passed_along(upper_layer, "gz", 1)
    own_layers = jnp.concatenate([stacked[:, 1:2] + from_below, stacked[:, 2 : size_z + 1]], axis=1)
    received = extended_2(own_layers, (("gx", 2), ("gy", 3)), 1)
    received = fold_rim(fold_rim(received, 2), 3)
    numerator = received[0]
    weight_sum = received[1]
    return (noisy + numerator) / (1.0 + weight_sum)


def solution(mesh):
    placed = (P("gz", "gx", "gy"),)
    return jax.shard_map(
        shards, mesh=mesh, in_specs=placed, out_specs=P("gz", "gx", "gy"), check_vma=False
    )
```

profile of v0, /device:TPU:42, one launch (start us, length us, event | category | flops | bytes accessed | tf_op | source)
XLA Modules:
  0.0 115.8 jit_solution(17542807814902700080)
XLA Ops:
  0.0 1.1 copy.99
  1.1 2.4 %collective-permute-start.1 = (f32[16,4,128]{2,0,1:T(8,128)S(1)}, f32[16,4,128]{2,0,1:T(8,128)S(1)}, u32[]{:S(2)}, u32[]{:S(2)}) collective-permute-start(f32[16,4,128]{2,0,1:T(8,128)S(1)} %get-tuple-element.64), channel_id=1, source_target_pairs={{64,0},{128,64},{192,128},{65,1},{129,65},{193,129},{66,2},{130,66... | collective-permute-start | bytes 98312 | tf_op jit(solution)/shard_map/ppermute | solution.py:24
  3.5 3.5 %collective-permute-start = (f32[16,4,128]{2,0,1:T(8,128)S(1)}, f32[16,4,128]{2,0,1:T(8,128)S(1)}, u32[]{:S(2)}, u32[]{:S(2)}) collective-permute-start(f32[16,4,128]{2,0,1:T(8,128)S(1)} %get-tuple-element.65), channel_id=1, source_target_pairs={{0,64},{64,128},{128,192},{1,65},{65,129},{129,193},{2,66},{66,130... | collective-permute-start | bytes 98312 | tf_op jit(solution)/shard_map/ppermute | solution.py:23
  7.1 2.2 %collective-permute-done = f32[16,4,128]{2,0,1:T(8,128)S(1)} collective-permute-done((f32[16,4,128]{2,0,1:T(8,128)S(1)}, f32[16,4,128]{2,0,1:T(8,128)S(1)}, u32[]{:S(2)}, u32[]{:S(2)}) %collective-permute-start) | collective-permute-done | bytes 32800 | tf_op jit(solution)/shard_map/ppermute | solution.py:23
  9.3 1.1 constant_dynamic-update-slice_fusion.1
  10.4 0.2 fusion.82
  10.6 8.2 %collective-permute-start.2 = (f32[16,40,4]{2,0,1:T(8,128)S(1)}, f32[16,40,4]{2,0,1:T(8,128)S(1)}, u32[]{:S(2)}, u32[]{:S(2)}) collective-permute-start(f32[16,40,4]{2,0,1:T(8,128)S(1)} %get-tuple-element.62), channel_id=1, source_target_pairs={{0,8},{8,16},{16,24},{24,32},{32,40},{40,48},{48,56},{1,9},{9,17},... | collective-permute-start | bytes 30728 | tf_op jit(solution)/shard_map/ppermute | solution.py:23
  18.8 2.5 %collective-permute-start.3 = (f32[16,40,4]{2,0,1:T(8,128)S(1)}, f32[16,40,4]{2,0,1:T(8,128)S(1)}, u32[]{:S(2)}, u32[]{:S(2)}) collective-permute-start(f32[16,40,4]{2,0,1:T(8,128)S(1)} %get-tuple-element.63), channel_id=1, source_target_pairs={{8,0},{16,8},{24,16},{32,24},{40,32},{48,40},{56,48},{9,1},{17,9},... | collective-permute-start | bytes 30728 | tf_op jit(solution)/shard_map/ppermute | solution.py:24
  21.3 13.2 %collective-permute-done.2 = f32[16,40,4]{2,0,1:T(8,128)S(1)} collective-permute-done((f32[16,40,4]{2,0,1:T(8,128)S(1)}, f32[16,40,4]{2,0,1:T(8,128)S(1)}, u32[]{:S(2)}, u32[]{:S(2)}) %collective-permute-start.2) | collective-permute-done | bytes 10272 | tf_op jit(solution)/shard_map/ppermute | solution.py:23
  34.5 7.3 %collective-permute-done.3 = f32[16,40,4]{2,0,1:T(8,128)S(1)} collective-permute-done((f32[16,40,4]{2,0,1:T(8,128)S(1)}, f32[16,40,4]{2,0,1:T(8,128)S(1)}, u32[]{:S(2)}, u32[]{:S(2)}) %collective-permute-start.3) | collective-permute-done | bytes 10272 | tf_op jit(solution)/shard_map/ppermute | solution.py:24
  41.8 0.3 pad_maximum_fusion.10
  42.1 1.9 %collective-permute-start.5 = (f32[4,40,136]{2,0,1:T(4,128)S(1)}, f32[4,40,136]{2,0,1:T(4,128)S(1)}, u32[]{:S(2)}, u32[]{:S(2)}) collective-permute-start(f32[4,40,136]{2,0,1:T(4,128)S(1)} %get-tuple-element.61), channel_id=1, source_target_pairs={{1,0},{2,1},{3,2},{4,3},{5,4},{6,5},{7,6},{9,8},{10,9},{11,10},{12... | collective-permute-start | bytes 261128 | tf_op jit(solution)/shard_map/ppermute | solution.py:24
  44.0 2.4 %collective-permute-start.4 = (f32[4,40,136]{2,0,1:T(4,128)S(1)}, f32[4,40,136]{2,0,1:T(4,128)S(1)}, u32[]{:S(2)}, u32[]{:S(2)}) collective-permute-start(f32[4,40,136]{2,0,1:T(4,128)S(1)} %get-tuple-element.60), channel_id=1, source_target_pairs={{0,1},{1,2},{2,3},{3,4},{4,5},{5,6},{6,7},{8,9},{9,10},{10,11},{11... | collective-permute-start | bytes 261128 | tf_op jit(solution)/shard_map/ppermute | solution.py:23
  46.5 0.2 broadcast_multiply_fusion
  46.6 0.7 collective-permute-done.5
  47.3 6.4 %collective-permute-done.4 = f32[4,40,136]{2,0,1:T(4,128)S(1)} collective-permute-done((f32[4,40,136]{2,0,1:T(4,128)S(1)}, f32[4,40,136]{2,0,1:T(4,128)S(1)}, u32[]{:S(2)}, u32[]{:S(2)}) %collective-permute-start.4) | collective-permute-done | bytes 87072 | tf_op jit(solution)/shard_map/ppermute | solution.py:23
  53.7 0.5 pad_maximum_fusion.3
  54.2 1.3 %fusion.21 = (f32[22,38,134]{2,0,1:T(8,128)S(1)}, f32[22,38,134]{2,0,1:T(8,128)S(1)}, f32[22,38,134]{2,0,1:T(8,128)S(1)}, f32[22,38,134]{2,0,1:T(8,128)S(1)}) fusion(f32[24,40,136]{2,0,1:T(8,128)S(1)} %pad_maximum_fusion.3), kind=kLoop, calls=%fused_computation.43 | loop fusion | flops 896192 | bytes 4032864 | tf_op jit(solution)/shard_map/mul | solution.py:60
  55.5 1.6 %fusion.20 = (f32[22,38,134]{2,0,1:T(8,128)S(1)}, f32[22,38,134]{2,0,1:T(8,128)S(1)}, f32[22,38,134]{2,0,1:T(8,128)S(1)}, f32[22,38,134]{2,0,1:T(8,128)S(1)}, f3...) fusion(f32[24,40,136]{2,0,1:T(8,128)S(1)} %pad_maximum_fusion.3), kind=kLoop, calls=%fused_computation.41 | loop fusion | flops 2016432 | bytes 8513824 | tf_op jit(solution)/shard_map/mul | solution.py:60
  57.0 0.7 slice_add_fusion.60
  57.9 0.4 slice_add_fusion.66
  58.3 0.1 slice_add_fusion.144
  58.4 0.7 slice_add_fusion.42
  59.2 0.1 slice_add_fusion.126
  59.5 0.7 slice_add_fusion
  60.3 0.7 slice_add_fusion.30
  61.3 0.7 slice_add_fusion.18
  62.3 0.7 slice_add_fusion.6
  63.4 0.8 copy-done
  64.2 0.6 copy_multiply_fusion
  64.8 1.0 copy_multiply_fusion.11
  65.8 1.2 copy_multiply_fusion.8
  66.9 1.0 copy_multiply_fusion.10
  68.0 1.0 copy_multiply_fusion.6
  68.9 1.0 copy_multiply_fusion.4
  70.0 1.0 copy_multiply_fusion.2
  71.0 0.2 add_add_fusion
  71.2 2.2 %add_bitcast_fusion = f32[1,18,34,130]{3,1,2,0:T(8,128)S(1)} fusion(f32[16,32,128]{2,0,1:T(8,128)S(1)} %add_add_fusion, f32[16,32,128]{2,0,1:T(8,128)S(1)} %get-tuple-element.30, f32[16,32,128]{2,0,1:T(8,128)S(1)} %get-tuple-element.46, f32[16,32,128]{2,0,1:T(8,128)S(1)} %get-tuple-element.26, f32[16,32,128]{2,0,1:T(8,128)S(1)} %get-tuple-element.44, ...), kind=kLoop, calls=%fused_computation.44 | loop fusion | flops 1034280 | bytes 3988256 | tf_op jit(solution)/shard_map/stack | solution.py:134
  73.4 0.3 pad_maximum_fusion.4
  73.7 1.1 fusion.27
  74.8 2.2 %add_bitcast_fusion.1 = f32[1,18,34,130]{3,1,2,0:T(8,128)S(1)} fusion(f32[16,32,128]{2,0,1:T(8,128)S(1)} %fusion.27, f32[16,32,128]{2,0,1:T(8,128)S(1)} %get-tuple-element.29, f32[16,32,128]{2,0,1:T(8,128)S(1)} %get-tuple-element.45, f32[16,32,128]{2,0,1:T(8,128)S(1)} %get-tuple-element.25, f32[16,32,128]{2,0,1:T(8,128)S(1)} %get-tuple-element.43, ...), kind=kLoop, calls=%fused_computation.45 | loop fusion | flops 1034280 | bytes 3988256 | tf_op jit(solution)/shard_map/stack | solution.py:134
  77.1 2.9 %collective-permute-start.6 = (f32[2,1,34,130]{3,1,2,0:T(1,128)S(1)}, f32[2,1,34,130]{3,1,2,0:T(1,128)S(1)}, u32[]{:S(2)}, u32[]{:S(2)}) collective-permute-start(f32[2,1,34,130]{3,1,2,0:T(1,128)S(1)} %pad_maximum_fusion.11), channel_id=1, source_target_pairs={{0,1},{1,2},{2,3},{3,4},{4,5},{5,6},{6,7},{8,9},{9,10},{10,11},{11... | collective-permute-start | bytes 106088 | tf_op jit(solution)/shard_map/ppermute | solution.py:32
  80.0 0.2 pad_maximum_fusion.2
  80.2 2.5 %collective-permute-done.6 = f32[2,1,34,130]{3,1,2,0:T(1,128)S(1)} collective-permute-done((f32[2,1,34,130]{3,1,2,0:T(1,128)S(1)}, f32[2,1,34,130]{3,1,2,0:T(1,128)S(1)}, u32[]{:S(2)}, u32[]{:S(2)}) %collective-permute-start.6) | collective-permute-done | bytes 35392 | tf_op jit(solution)/shard_map/ppermute | solution.py:32
  82.9 3.5 %collective-permute-start.7 = (f32[2,16,1,130]{3,1,2,0:T(8,128)S(1)}, f32[2,16,1,130]{3,1,2,0:T(8,128)S(1)}, u32[]{:S(2)}, u32[]{:S(2)}) collective-permute-start(f32[2,16,1,130]{3,1,2,0:T(8,128)S(1)} %get-tuple-element.31), channel_id=1, source_target_pairs={{0,64},{64,128},{128,192},{1,65},{65,129},{129,193},{2,66},{66,130... | collective-permute-start | bytes 49928 | tf_op jit(solution)/shard_map/ppermute | solution.py:23
  86.3 2.4 %collective-permute-start.8 = (f32[2,16,1,130]{3,1,2,0:T(8,128)S(1)}, f32[2,16,1,130]{3,1,2,0:T(8,128)S(1)}, u32[]{:S(2)}, u32[]{:S(2)}) collective-permute-start(f32[2,16,1,130]{3,1,2,0:T(8,128)S(1)} %get-tuple-element.32), channel_id=1, source_target_pairs={{64,0},{128,64},{192,128},{65,1},{129,65},{193,129},{66,2},{130,66... | collective-permute-start | bytes 49928 | tf_op jit(solution)/shard_map/ppermute | solution.py:24
  88.7 0.1 collective-permute-done.7
  88.9 3.5 %collective-permute-done.8 = f32[2,16,1,130]{3,1,2,0:T(8,128)S(1)} collective-permute-done((f32[2,16,1,130]{3,1,2,0:T(8,128)S(1)}, f32[2,16,1,130]{3,1,2,0:T(8,128)S(1)}, u32[]{:S(2)}, u32[]{:S(2)}) %collective-permute-start.8) | collective-permute-done | bytes 16672 | tf_op jit(solution)/shard_map/ppermute | solution.py:24
  92.4 0.2 pad_maximum_fusion
  92.6 0.2 fusion.81
  92.8 0.3 copy.95
  93.1 9.7 %collective-permute-start.9 = (f32[2,16,36,1]{2,1,3,0:T(8,128)S(1)}, f32[2,16,36,1]{2,1,3,0:T(8,128)S(1)}, u32[]{:S(2)}, u32[]{:S(2)}) collective-permute-start(f32[2,16,36,1]{2,1,3,0:T(8,128)S(1)} %copy.95), channel_id=1, source_target_pairs={{0,8},{8,16},{16,24},{24,32},{32,40},{40,48},{48,56},{1,9},{9,17},... | collective-permute-start | bytes 13832 | tf_op jit(solution)/shard_map/ppermute | solution.py:23
  102.8 0.3 copy.96
  103.2 1.9 %collective-permute-start.10 = (f32[2,16,36,1]{2,1,3,0:T(8,128)S(1)}, f32[2,16,36,1]{2,1,3,0:T(8,128)S(1)}, u32[]{:S(2)}, u32[]{:S(2)}) collective-permute-start(f32[2,16,36,1]{2,1,3,0:T(8,128)S(1)} %copy.96), channel_id=1, source_target_pairs={{8,0},{16,8},{24,16},{32,24},{40,32},{48,40},{56,48},{9,1},{17,9},... | collective-permute-start | bytes 13832 | tf_op jit(solution)/shard_map/ppermute | solution.py:24
  105.1 0.4 copy.97
  105.5 7.2 %collective-permute-done.10 = f32[2,16,36,1]{2,1,3,0:T(8,128)S(1)} collective-permute-done((f32[2,16,36,1]{2,1,3,0:T(8,128)S(1)}, f32[2,16,36,1]{2,1,3,0:T(8,128)S(1)}, u32[]{:S(2)}, u32[]{:S(2)}) %collective-permute-start.10) | collective-permute-done | bytes 4640 | tf_op jit(solution)/shard_map/ppermute | solution.py:24
  112.7 0.4 copy.98
  113.1 0.7 pad_maximum_fusion.1
  113.8 0.1 fusion
  114.0 0.2 slice.1682
  114.2 0.3 copy-done.1
  114.5 0.3 fusion.23
  114.8 0.2 fusion.25
  115.0 0.8 copy.100
  (27 shorter events, 1.6 us)
Async XLA Ops:
  1.1 9.3 %collective-permute-start.1 = (f32[16,4,128]{2,0,1:T(8,128)S(1)}, f32[16,4,128]{2,0,1:T(8,128)S(1)}, u32[]{:S(2)}, u32[]{:S(2)}) collective-permute-start(f32[16,4,128]{2,0,1:T(8,128)S(1)} %get-tuple-element.64), channel_id=1, source_target_pairs={{64,0},{128,64},{192,128},{65,1},{129,65},{193,129},{66,2},{130,66... | collective-permute-start | bytes 98312 | tf_op jit(solution)/shard_map/ppermute | solution.py:24
  3.5 5.8 %collective-permute-start = (f32[16,4,128]{2,0,1:T(8,128)S(1)}, f32[16,4,128]{2,0,1:T(8,128)S(1)}, u32[]{:S(2)}, u32[]{:S(2)}) collective-permute-start(f32[16,4,128]{2,0,1:T(8,128)S(1)} %get-tuple-element.65), channel_id=1, source_target_pairs={{0,64},{64,128},{128,192},{1,65},{65,129},{129,193},{2,66},{66,130... | collective-permute-start | bytes 98312 | tf_op jit(solution)/shard_map/ppermute | solution.py:23
  10.6 23.9 %collective-permute-start.2 = (f32[16,40,4]{2,0,1:T(8,128)S(1)}, f32[16,40,4]{2,0,1:T(8,128)S(1)}, u32[]{:S(2)}, u32[]{:S(2)}) collective-permute-start(f32[16,40,4]{2,0,1:T(8,128)S(1)} %get-tuple-element.62), channel_id=1, source_target_pairs={{0,8},{8,16},{16,24},{24,32},{32,40},{40,48},{48,56},{1,9},{9,17},... | collective-permute-start | bytes 30728 | tf_op jit(solution)/shard_map/ppermute | solution.py:23
  18.8 23.0 %collective-permute-start.3 = (f32[16,40,4]{2,0,1:T(8,128)S(1)}, f32[16,40,4]{2,0,1:T(8,128)S(1)}, u32[]{:S(2)}, u32[]{:S(2)}) collective-permute-start(f32[16,40,4]{2,0,1:T(8,128)S(1)} %get-tuple-element.63), channel_id=1, source_target_pairs={{8,0},{16,8},{24,16},{32,24},{40,32},{48,40},{56,48},{9,1},{17,9},... | collective-permute-start | bytes 30728 | tf_op jit(solution)/shard_map/ppermute | solution.py:24
  42.1 5.2 %collective-permute-start.5 = (f32[4,40,136]{2,0,1:T(4,128)S(1)}, f32[4,40,136]{2,0,1:T(4,128)S(1)}, u32[]{:S(2)}, u32[]{:S(2)}) collective-permute-start(f32[4,40,136]{2,0,1:T(4,128)S(1)} %get-tuple-element.61), channel_id=1, source_target_pairs={{1,0},{2,1},{3,2},{4,3},{5,4},{6,5},{7,6},{9,8},{10,9},{11,10},{12... | collective-permute-start | bytes 261128 | tf_op jit(solution)/shard_map/ppermute | solution.py:24
  44.0 9.7 %collective-permute-start.4 = (f32[4,40,136]{2,0,1:T(4,128)S(1)}, f32[4,40,136]{2,0,1:T(4,128)S(1)}, u32[]{:S(2)}, u32[]{:S(2)}) collective-permute-start(f32[4,40,136]{2,0,1:T(4,128)S(1)} %get-tuple-element.60), channel_id=1, source_target_pairs={{0,1},{1,2},{2,3},{3,4},{4,5},{5,6},{6,7},{8,9},{9,10},{10,11},{11... | collective-permute-start | bytes 261128 | tf_op jit(solution)/shard_map/ppermute | solution.py:23
  63.3 1.0 copy-start
  77.1 5.6 %collective-permute-start.6 = (f32[2,1,34,130]{3,1,2,0:T(1,128)S(1)}, f32[2,1,34,130]{3,1,2,0:T(1,128)S(1)}, u32[]{:S(2)}, u32[]{:S(2)}) collective-permute-start(f32[2,1,34,130]{3,1,2,0:T(1,128)S(1)} %pad_maximum_fusion.11), channel_id=1, source_target_pairs={{0,1},{1,2},{2,3},{3,4},{4,5},{5,6},{6,7},{8,9},{9,10},{10,11},{11... | collective-permute-start | bytes 106088 | tf_op jit(solution)/shard_map/ppermute | solution.py:32
  82.9 6.0 %collective-permute-start.7 = (f32[2,16,1,130]{3,1,2,0:T(8,128)S(1)}, f32[2,16,1,130]{3,1,2,0:T(8,128)S(1)}, u32[]{:S(2)}, u32[]{:S(2)}) collective-permute-start(f32[2,16,1,130]{3,1,2,0:T(8,128)S(1)} %get-tuple-element.31), channel_id=1, source_target_pairs={{0,64},{64,128},{128,192},{1,65},{65,129},{129,193},{2,66},{66,130... | collective-permute-start | bytes 49928 | tf_op jit(solution)/shard_map/ppermute | solution.py:23
  86.3 6.0 %collective-permute-start.8 = (f32[2,16,1,130]{3,1,2,0:T(8,128)S(1)}, f32[2,16,1,130]{3,1,2,0:T(8,128)S(1)}, u32[]{:S(2)}, u32[]{:S(2)}) collective-permute-start(f32[2,16,1,130]{3,1,2,0:T(8,128)S(1)} %get-tuple-element.32), channel_id=1, source_target_pairs={{64,0},{128,64},{192,128},{65,1},{129,65},{193,129},{66,2},{130,66... | collective-permute-start | bytes 49928 | tf_op jit(solution)/shard_map/ppermute | solution.py:24
  93.1 11.9 %collective-permute-start.9 = (f32[2,16,36,1]{2,1,3,0:T(8,128)S(1)}, f32[2,16,36,1]{2,1,3,0:T(8,128)S(1)}, u32[]{:S(2)}, u32[]{:S(2)}) collective-permute-start(f32[2,16,36,1]{2,1,3,0:T(8,128)S(1)} %copy.95), channel_id=1, source_target_pairs={{0,8},{8,16},{16,24},{24,32},{32,40},{40,48},{48,56},{1,9},{9,17},... | collective-permute-start | bytes 13832 | tf_op jit(solution)/shard_map/ppermute | solution.py:23
  103.2 9.5 %collective-permute-start.10 = (f32[2,16,36,1]{2,1,3,0:T(8,128)S(1)}, f32[2,16,36,1]{2,1,3,0:T(8,128)S(1)}, u32[]{:S(2)}, u32[]{:S(2)}) collective-permute-start(f32[2,16,36,1]{2,1,3,0:T(8,128)S(1)} %copy.96), channel_id=1, source_target_pairs={{8,0},{16,8},{24,16},{32,24},{40,32},{48,40},{56,48},{9,1},{17,9},... | collective-permute-start | bytes 13832 | tf_op jit(solution)/shard_map/ppermute | solution.py:24
  113.1 0.7 copy-start.2
  113.8 0.7 copy-start.1
where the time goes:
time: 116 us
  waiting for transfers between devices  43.2 us (37%)
  starting transfers between devices  41.2 us (36%)
  other arithmetic  24.7 us (21%)
  local copies, waits for them, and re-layouts  6.16 us (5%)
    ppermute x5, starting transfers between devices, extended_2(): before = lax.ppermute(last, axis, up)  27.2 us
    ppermute x5, waiting for transfers between devices, extended_2(): before = lax.ppermute(last, axis, up)  22 us
    ppermute x5, waiting for transfers between devices, extended_2(): after = lax.ppermute(leading, axis, down)  18.7 us
    ppermute x5, starting transfers between devices, extended_2(): after = lax.ppermute(leading, axis, down)  11 us
    mul x7, other arithmetic, shards(): credit_num = credit_num + place_shifted(weights * noisy, offset)  6.7 us
    add x7, other arithmetic, box_sum(): total = total + field[shift_by:shift_by + length]  4.72 us
    another operation x3, other arithmetic, shards(): stacked = jnp.stack([numerator, weight_sum])  4.53 us
    unnamed x9, local copies, waits for them, and re-layouts  3.34 us
  transfers between devices with their start and end apart: 11, of which 9 were waited for; matrix products, arithmetic and copies ran while one was open for 2% of the time, Pallas kernels for 0%

commit v1 on v0

v1 whole, which is shorter than its diff:
```python
import functools
import math

import jax
import jax.numpy as jnp
import ml_dtypes
import numpy as np
from jax import lax
from jax.experimental import pallas as pl
from jax.experimental.pallas import tpu as pltpu
from jax.sharding import PartitionSpec as P

GROUPS = ((0, 0), (0, 1), (1, -1), (1, 0), (1, 1))
VARIANTS = tuple((dz, dx) for dz in (-1, 0, 1) for dx in (-1, 0, 1))
SCALE = math.sqrt(math.log2(math.e) / 343.0)
SZ, SX, SY = 16, 32, 128
BASE, PITCH = 16, 64
MASKED = -1000.0
MESH = pl.DeviceIdType.MESH
F32, BF16 = jnp.float32, jnp.bfloat16


def box_tables():
    n = np.arange(256)
    k = np.arange(512)
    j = np.arange(256)
    zk, xk = k // 32, k % 32
    zj, s = j // 8, j % 8
    xj = np.where(s < 4, 32 + s, s - 8)
    planes, rims = [], []
    for dz, dx in GROUPS:
        xc = n % 32 - dx
        zc = 4 + n // 32 - dz
        near = (abs(zk[:, None] - zc) <= 3) & (abs(xk[:, None] - xc) <= 3)
        planes.append(-near.astype(np.float32))
        halves = []
        for half in range(2):
            near = (abs(zj[:, None] - zc - 8 * half) <= 3) & (abs(xj[:, None] - xc) <= 3) & (j < 192)[:, None]
            halves.append(-near.astype(np.float32))
        rims.append(np.stack(halves))
    return np.stack(planes).astype(ml_dtypes.bfloat16), np.stack(rims).astype(ml_dtypes.bfloat16)


def iota(shape, dim):
    return lax.broadcasted_iota(jnp.int32, shape, dim)


def kernel(x_ref, wp_hbm, wh_hbm, out_ref, ext, xs_lo, xs_hi, xp, xm, ys_lo, ys_hi, yr_lo, yr_hi,
           shifted, rows_h, wp, wh, lhs, dist, num, wsum, local_sem, send_sem, recv_sem):
    gx, gy, gz = lax.axis_index("gx"), lax.axis_index("gy"), lax.axis_index("gz")
    nx, ny, nz = lax.axis_size("gx"), lax.axis_size("gy"), lax.axis_size("gz")

    own = pltpu.make_async_copy(x_ref, ext.at[pl.ds(4, SZ), pl.ds(BASE, SX), :], local_sem.at[0])
    own.start()
    tables = [pltpu.make_async_copy(wp_hbm, wp, local_sem.at[1]), pltpu.make_async_copy(wh_hbm, wh, local_sem.at[2])]
    for copy in tables:
        copy.start()

    ext[0:4] = jnp.zeros((4, PITCH, 128), F32)
    ext[20:26] = jnp.zeros((6, PITCH, 128), F32)
    ext[4:20, 0:BASE] = jnp.zeros((SZ, BASE, 128), F32)
    ext[4:20, BASE + SX:PITCH] = jnp.zeros((SZ, PITCH - BASE - SX, 128), F32)
    xp[...] = jnp.zeros_like(xp)
    xm[...] = jnp.zeros_like(xm)
    yr_lo[...] = jnp.zeros_like(yr_lo)
    yr_hi[...] = jnp.zeros_like(yr_hi)

    z_ok = {-1: gz > 0, 0: True, 1: gz < nz - 1}
    x_ok = {-1: gx > 0, 0: True, 1: gx < nx - 1}
    y_ok = {-1: gy > 0, 1: gy < ny - 1}

    def both(a, b):
        if a is True:
            return b
        if b is True:
            return a
        return jnp.logical_and(a, b)

    barrier = pltpu.get_barrier_semaphore()
    around = [(dz, dx) for dz in (-1, 0, 1) for dx in (-1, 0, 1) if (dz, dx) != (0, 0)]
    for dz, dx in around:
        @pl.when(both(z_ok[dz], x_ok[dx]))
        def _():
            pl.semaphore_signal(barrier, inc=1, device_id=(gx + dx, gy, gz + dz), device_id_type=MESH)
    for dy in (-1, 1):
        @pl.when(y_ok[dy])
        def _():
            pl.semaphore_signal(barrier, inc=1, device_id=(gx, gy + dy, gz), device_id_type=MESH)

    def count(ok):
        return ok[-1].astype(jnp.int32) + ok[1].astype(jnp.int32)

    own.wait()
    xs_lo[...] = ext[4:20, BASE:BASE + 4, :]
    xs_hi[...] = ext[4:20, BASE + 28:BASE + 32, :]
    pl.semaphore_wait(barrier, (1 + count(z_ok)) * (1 + count(x_ok)) - 1 + count(y_ok))

    def parts(dz, dx):
        send_z = {-1: slice(0, 4), 0: slice(0, 16), 1: slice(12, 16)}[dz]
        land_z = {-1: slice(20, 24), 0: slice(4, 20), 1: slice(0, 4)}[dz]
        send_z = pl.ds(send_z.start, send_z.stop - send_z.start)
        land_z = pl.ds(land_z.start, land_z.stop - land_z.start)
        if dx == 0:
            return x_ref.at[send_z], ext.at[land_z, pl.ds(BASE, SX), :]
        if dx == -1:
            return xs_lo.at[send_z], xp.at[land_z]
        return xs_hi.at[send_z], xm.at[land_z]

    copies = []
    for i, (dz, dx) in enumerate(around):
        src, dst = parts(dz, dx)
        copy = pltpu.make_async_remote_copy(
            src_ref=src, dst_ref=dst, send_sem=send_sem.at[i], recv_sem=recv_sem.at[i],
            device_id=(gx + dx, gy, gz + dz), device_id_type=MESH)
        copies.append((copy, dz, dx))
        pl.when(both(z_ok[dz], x_ok[dx]))(copy.start)
    for copy, dz, dx in copies:
        pl.when(both(z_ok[-dz], x_ok[-dx]))(copy.wait_recv)
    ext[0:24, BASE + 32:BASE + 36, :] = xp[...]
    ext[0:24, BASE - 4:BASE, :] = xm[...]

    lane = iota((128, 128), 1)
    low_half = iota((8, 128), 0) < 4

    def block(v, k):
        dz, dx = VARIANTS[v]
        if k < 6:
            return jnp.concatenate([ext[4 * k + j + dz, BASE + dx:BASE + 32 + dx, :] for j in range(4)], axis=0)
        pieces = []
        for j in range(16 if k == 6 else 8):
            zi = 16 * (k - 6) + j + dz
            pieces.append(jnp.where(low_half, ext[zi, BASE + 32 + dx:BASE + 40 + dx, :], ext[zi, BASE - 8 + dx:BASE + dx, :]))
        if k == 7:
            pieces.append(jnp.zeros((64, 128), F32))
        return jnp.concatenate(pieces, axis=0)

    def place(v, k):
        turned = (block(v, k) * SCALE).T
        if k == 7 and v > 4:
            turned = jnp.where(lane == 64 + v - 4, 1.0, turned)
        for c in range(8):
            shifted[v, k, pl.ds(8 + c, 16, stride=8), :] = turned[16 * c:16 * c + 16]
        return turned

    for k in range(8):
        turned = place(4, k)
        ys_lo[k] = turned[0:4]
        ys_hi[k] = turned[124:128]
    y_copies = []
    for i, (dy, src, dst) in enumerate(((-1, ys_lo, yr_hi), (1, ys_hi, yr_lo))):
        copy = pltpu.make_async_remote_copy(
            src_ref=src, dst_ref=dst, send_sem=send_sem.at[8 + i], recv_sem=recv_sem.at[8 + i],
            device_id=(gx, gy + dy, gz), device_id_type=MESH)
        y_copies.append((copy, dy))
        pl.when(y_ok[dy])(copy.start)
    for v in range(9):
        if v != 4:
            for k in (range(8) if v > 4 else range(1, 5)):
                place(v, k)

    for copy in tables:
        copy.wait()
    row = iota((16, 256), 0)
    col = iota((16, 256), 1)
    row_dz = jnp.where(row >= 2, 1, 0)
    row_dx = jnp.where(row == 1, 1, jnp.where((row >= 2) & (row < 5), row - 3, 0))
    known = (row >= 1) & (row < 5)
    for half in range(2):
        vz = gz * SZ + 8 * half + col // 32
        vx = gx * SX + col % 32

        def outside(sign):
            z, x = vz + sign * row_dz, vx + sign * row_dx
            return (z < 0) | (z >= nz * SZ) | (x < 0) | (x >= nx * SX)

        wh[0, half, 192:208, :] = jnp.where(known & outside(1), MASKED, 0.0).astype(BF16)
        back = known & outside(-1)
        for g in range(1, 5):
            wh[g, half, 192:208, :] = jnp.where(back & (row == g), MASKED, 0.0).astype(BF16)

    for copy, dy in y_copies:
        pl.when(y_ok[-dy])(copy.wait_recv)
    for i in range(4):
        for k in range(8):
            rows_h[4, k, (2 + 2 * i) % 8:(2 + 2 * i) % 8 + 1, :] = yr_lo[k, i:i + 1, :]
            rows_h[4, k, 7 - 2 * i:8 - 2 * i, :] = yr_hi[k, i:i + 1, :]
    lane8 = iota((8, 128), 1)
    sub = iota((8, 128), 0)

    def turn(value, by, axis):
        by = by % value.shape[axis]
        return value if by == 0 else pltpu.roll(value, by, axis)

    for dx in (-1, 1):
        v = 4 + dx
        for k in range(6):
            value = turn(rows_h[4, k], -dx, 1)
            edge = 31 if dx == 1 else 0
            source = rows_h[4, 6 + k // 4]
            for j in range(4):
                src_lane = (4 * (k % 4) + j) * 8 + (0 if dx == 1 else 7)
                dst_lane = 32 * j + edge
                value = jnp.where(lane8 == dst_lane, turn(source, dst_lane - src_lane, 1), value)
            rows_h[v, k] = value
        for m in range(2):
            value = turn(rows_h[4, 6 + m], -dx, 1)
            for zz in range(16 if m == 0 else 8):
                k = 4 * m + zz // 4
                src_lane = 32 * (zz % 4) + (0 if dx == 1 else 31)
                dst_lane = 8 * zz + (7 if dx == 1 else 0)
                value = jnp.where(lane8 == dst_lane, turn(rows_h[4, k], dst_lane - src_lane, 1), value)
            rows_h[v, 6 + m] = value
    for dx in (-1, 0, 1):
        for k in range(6):
            here = turn(rows_h[4 + dx, k], -32, 1)
            after = turn(rows_h[4 + dx, k + 1], -32, 1) if k < 5 else here
            rows_h[7 + dx, k] = jnp.where(lane8 < 96, here, after)
            if 1 <= k <= 4:
                here = turn(rows_h[4 + dx, k], 32, 1)
                before = turn(rows_h[4 + dx, k - 1], 32, 1)
                rows_h[1 + dx, k] = jnp.where(lane8 >= 32, here, before)
        here, after = turn(rows_h[4 + dx, 6], -8, 1), turn(rows_h[4 + dx, 7], -8, 1)
        rows_h[7 + dx, 6] = jnp.where(lane8 < 120, here, after)
        rows_h[7 + dx, 7] = after
    for v in range(5, 9):
        rows_h[v, 7] = jnp.where(lane8 >= 64, jnp.where(lane8 == 64 + v - 4, 1.0, 0.0), rows_h[v, 7])
    rows_h[4, 7] = jnp.where(lane8 >= 64, 0.0, rows_h[4, 7])

    for v in range(9):
        for k in (range(8) if v >= 4 else range(1, 5)):
            shifted[v, k, 0:8, :] = jnp.where(sub == 0, rows_h[v, k], turn(shifted[v, k, 128:136, :], 1, 0))
            shifted[v, k, 136:144, :] = jnp.where(sub == 7, rows_h[v, k], turn(shifted[v, k, 8:16, :], -1, 0))

    odd = sub % 2 == 1

    def halo_rows(v, k, dy):
        value = rows_h[v, k]
        if dy == 0:
            return value
        up, down = turn(value, 2, 0), turn(value, -2, 0)
        if dy == 1:
            return jnp.where(odd, up, jnp.where(sub == 0, shifted[v, k, 8:16, :], down))
        return jnp.where(odd, jnp.where(sub == 7, shifted[v, k, 128:136, :], down), up)

    def build(g, dys):
        v = g + 4
        for d, dy in enumerate(dys):
            for k in range(8):
                lanes = slice(128 * k, 128 * k + 128)
                error = None
                for j in range(8):
                    diff = shifted[4, k, 8 + 16 * j:24 + 16 * j, :] - shifted[v, k, 8 + 16 * j + 8 * dy:24 + 16 * j + 8 * dy, :]
                    square = diff * diff
                    if error is not None:
                        square = square + error
                    rounded = square.astype(BF16)
                    lhs[128 * d + 16 * j:128 * d + 16 * j + 16, lanes] = rounded
                    error = square - rounded.astype(F32)
                diff = rows_h[4, k] - halo_rows(v, k, dy)
                square = diff * diff
                high = square.astype(BF16).astype(F32)
                at = 128 * len(dys) + 16 * d
                lhs[at:at + 16, lanes] = jnp.concatenate([high, square - high], axis=0).astype(BF16)

    def multiply(g, rows):
        for w, table in enumerate((0, g)):
            if w == 1 and g == 0:
                continue
            for half in range(2):
                total = jnp.dot(lhs[0:rows, 256 * half:256 * half + 512], wp[table], preferred_element_type=F32)
                total = total + jnp.dot(lhs[0:rows, 768:1024], wh[table, half], preferred_element_type=F32)
                dist[w, 0:rows, 256 * half:256 * half + 256] = total

    keep_lo = jnp.where((sub == 0) & (gy == 0), 0.0, 1.0)
    keep_hi = jnp.where((sub == 7) & (gy == ny - 1), 0.0, 1.0)

    def weights(w, d, at, n, first):
        lanes = slice(128 * n, 128 * n + 128)
        halo = dist[w, at:at + 8, lanes] + dist[w, at + 8:at + 16, lanes]
        cache = {}

        def get(t):
            if t in cache:
                return cache[t]
            if 0 <= t < 16:
                value = dist[w, 128 * d + 8 * t:128 * d + 8 * t + 8, lanes]
            elif t < 0:
                value = jnp.where(sub == 0, turn(halo, 2 * (-t - 1), 0), turn(get(16 + t), 1, 0))
            else:
                value = jnp.where(sub == 7, turn(halo, 2 * (t - 16), 0), turn(get(t - 16), -1, 0))
            cache[t] = value
            return value

        total = get(first - 3)
        for t in range(first - 2, first + 4):
            total = total + get(t)
        result = [jnp.exp2(total)]
        for t in range(first + 1, first + 16):
            total = total + (get(t + 3) - get(t - 4))
            result.append(jnp.exp2(total))
        return result

    def gather(g, dys, start):
        v = g + 4
        for n in range(4):
            lanes = slice(128 * n, 128 * n + 128)
            for d, dy in enumerate(dys):
                at = 128 * len(dys) + 16 * d
                ahead = weights(0, d, at, n, 0)
                behind = weights(1 if g else 0, d, at, n, -dy)
                if dy == 1:
                    ahead[15] = ahead[15] * keep_hi
                    behind[0] = behind[0] * keep_lo
                elif dy == -1:
                    ahead[0] = ahead[0] * keep_lo
                    behind[15] = behind[15] * keep_hi
                for t in range(16):
                    rows = slice(8 * t, 8 * t + 8)
                    up = shifted[v, n + 1, 8 + 8 * (t + dy):16 + 8 * (t + dy), :]
                    down = shifted[8 - v, n + 1, 8 + 8 * (t - dy):16 + 8 * (t - dy), :]
                    part = ahead[t] * up + behind[t] * down
                    part_w = ahead[t] + behind[t]
                    if start and d == 0:
                        num[rows, lanes] = part
                        wsum[rows, lanes] = part_w
                    else:
                        num[rows, lanes] += part
                        wsum[rows, lanes] += part_w

    for g in range(5):
        dys = (1,) if g == 0 else (-1, 0, 1)
        build(g, dys)
        multiply(g, 144 * len(dys))
        gather(g, dys, g == 0)

    for n in range(4):
        lanes = slice(128 * n, 128 * n + 128)
        top = shifted[4, n + 1, 8:136, :] + num[:, lanes]
        shifted[0, n + 1, 8:136, :] = top * (1.0 / SCALE) / (1.0 + wsum[:, lanes])
        ordered = jnp.concatenate([shifted[0, n + 1, pl.ds(8 + c, 16, stride=8), :] for c in range(8)], axis=0)
        out_ref[4 * n:4 * n + 4] = ordered.T.reshape(4, 32, 128)

    for copy, dz, dx in copies:
        pl.when(both(z_ok[dz], x_ok[dx]))(copy.wait_send)
    for copy, dy in y_copies:
        pl.when(y_ok[dy])(copy.wait_send)


def shards(planes, rims, noisy):
    return pl.pallas_call(
        kernel,
        out_shape=jax.ShapeDtypeStruct(noisy.shape, F32),
        in_specs=[pl.BlockSpec(memory_space=pl.ANY)] * 3,
        out_specs=pl.BlockSpec(memory_space=pltpu.VMEM),
        scratch_shapes=[
            pltpu.VMEM((26, PITCH, 128), F32),
            pltpu.VMEM((16, 4, 128), F32),
            pltpu.VMEM((16, 4, 128), F32),
            pltpu.VMEM((24, 4, 128), F32),
            pltpu.VMEM((24, 4, 128), F32),
            pltpu.VMEM((8, 4, 128), F32),
            pltpu.VMEM((8, 4, 128), F32),
            pltpu.VMEM((8, 4, 128), F32),
            pltpu.VMEM((8, 4, 128), F32),
            pltpu.VMEM((9, 8, 144, 128), F32),
            pltpu.VMEM((9, 8, 8, 128), F32),
            pltpu.VMEM((5, 512, 256), BF16),
            pltpu.VMEM((5, 2, 256, 256), BF16),
            pltpu.VMEM((432, 1024), BF16),
            pltpu.VMEM((2, 432, 512), F32),
            pltpu.VMEM((128, 512), F32),
            pltpu.VMEM((128, 512), F32),
            pltpu.SemaphoreType.DMA((3,)),
            pltpu.SemaphoreType.DMA((10,)),
            pltpu.SemaphoreType.DMA((10,)),
        ],
        compiler_params=pltpu.CompilerParams(collective_id=0, has_side_effects=True, vmem_limit_bytes=56 << 20),
    )(noisy, jnp.asarray(planes), jnp.asarray(rims))


def solution(mesh):
    planes, rims = box_tables()
    placed = P("gz", "gx", "gy")
    return jax.shard_map(
        functools.partial(shards, planes, rims), mesh=mesh, in_specs=(placed,), out_specs=placed, check_vma=False
    )
```

time: 116 us -> 23.6 us (0.20)
  the two profiles are of different devices: /device:TPU:42 before, /device:TPU:1 now
where the time goes in v1:
time: 23.6 us; the launch traced here: 23.4 us
  Pallas kernels  21.7 us (92%)
  local copies, waits for them, and re-layouts  1.67 us (7%)
    pallas_call x1, Pallas kernels, shards(): pl.pallas_call(kernel, out_shape=jax.ShapeDtypeStruct(noisy.shape, F32),...  21.7 us
    unnamed x1, local copies, waits for them, and re-layouts  1.67 us

profile of v1, /device:TPU:1, one launch (start us, length us, event | category | flops | bytes accessed | tf_op | source)
XLA Modules:
  0.0 23.4 jit_solution(7411905738160009870)
XLA Ops:
  0.0 21.7 %shard_map.37 = f32[16,32,128]{2,1,0:T(8,128)} custom-call(f32[16,32,128]{2,1,0:T(8,128)} %x_ref.1, bf16[5,512,256]{2,1,0:T(8,128)(2,1)} %constant.4.clone.wp_hbm, bf16[5,2,256,256]{3,2,1,0:T(8,128)(2,1)} %constant.5.clone.wh_hbm), custom_call_target="tpu_custom_call" | custom-call | tf_op jit(solution)/shard_map/pallas_call | solution.py:350
  21.7 1.7 %copy.5 = f32[16,32,128]{2,1,0:T(8,128)} copy(f32[16,32,128]{2,1,0:T(8,128)} %shard_map.37) | data formatting | bytes 524288

commit v2 on v1

v2 whole, which is shorter than its diff:
```python
import functools
import math

import jax
import jax.numpy as jnp
import ml_dtypes
import numpy as np
from jax import lax
from jax.experimental import pallas as pl
from jax.experimental.pallas import tpu as pltpu
from jax.sharding import PartitionSpec as P

GROUPS = ((0, 0), (0, 1), (1, -1), (1, 0), (1, 1))
VARIANTS = tuple((dz, dx) for dz in (-1, 0, 1) for dx in (-1, 0, 1))
SCALE = math.sqrt(math.log2(math.e) / 343.0)
SZ, SX, SY = 16, 32, 128
BASE, PITCH = 16, 64
MASKED = -1000.0
MESH = pl.DeviceIdType.MESH
F32, BF16 = jnp.float32, jnp.bfloat16


def box_tables():
    n = np.arange(256)
    k = np.arange(512)
    j = np.arange(256)
    zk, xk = k // 32, k % 32
    zj, s = j // 8, j % 8
    xj = np.where(s < 4, 32 + s, s - 8)
    planes, rims = [], []
    for dz, dx in GROUPS:
        xc = n % 32 - dx
        zc = 4 + n // 32 - dz
        near = (abs(zk[:, None] - zc) <= 3) & (abs(xk[:, None] - xc) <= 3)
        planes.append(-near.astype(np.float32))
        halves = []
        for half in range(2):
            near = (abs(zj[:, None] - zc - 8 * half) <= 3) & (abs(xj[:, None] - xc) <= 3) & (j < 192)[:, None]
            halves.append(-near.astype(np.float32))
        rims.append(np.stack(halves))
    return np.stack(planes).astype(ml_dtypes.bfloat16), np.stack(rims).astype(ml_dtypes.bfloat16)


def iota(shape, dim):
    return lax.broadcasted_iota(jnp.int32, shape, dim)


def kernel(x_ref, wp_hbm, wh_hbm, out_ref, ext, xs_lo, xs_hi, xp, xm, ys_lo, ys_hi, yp_lo, yp_hi, yx_lo, yx_hi,
           ye_lo, ye_hi, yr_lo, yr_hi, shifted, rows_h, wp, wh, lhs, dist, num, wsum, lhs_h, dist_h, edge, edge_p, ordered, local_sem, send_sem, recv_sem, ready):
    gx, gy, gz = lax.axis_index("gx"), lax.axis_index("gy"), lax.axis_index("gz")
    nx, ny, nz = lax.axis_size("gx"), lax.axis_size("gy"), lax.axis_size("gz")
    even = gy % 2 == 0
    odd_side = gy % 2 == 1

    def there(dz, dx, dy):
        ok = None
        for at, size, step in ((gz, nz, dz), (gx, nx, dx), (gy, ny, dy)):
            if step:
                inside = at > 0 if step < 0 else at < size - 1
                ok = inside if ok is None else jnp.logical_and(ok, inside)
        return ok

    def device(dz, dx, dy):
        return (gx + dx, gy + dy, gz + dz)

    around = [(dz, dx) for dz in (-1, 0, 1) for dx in (-1, 0, 1)]
    beside = [o for o in around if o != (0, 0)]
    barrier = pltpu.get_barrier_semaphore()
    for dy in (-1, 1):
        for dz, dx in around:
            @pl.when(jnp.logical_and(even, there(dz, dx, dy)))
            def _():
                pl.semaphore_signal(barrier, inc=1, device_id=device(dz, dx, dy), device_id_type=MESH)
    for dz, dx in beside:
        @pl.when(there(dz, dx, 0))
        def _():
            pl.semaphore_signal(barrier, inc=1, device_id=device(dz, dx, 0), device_id_type=MESH)

    def count(at, size):
        return (at > 0).astype(jnp.int32) + (at < size - 1).astype(jnp.int32)

    n_plane = (1 + count(gz, nz)) * (1 + count(gx, nx))
    n_beside = count(gy, ny)
    n_across = n_plane * n_beside

    own = pltpu.make_async_copy(x_ref, ext.at[pl.ds(4, SZ), pl.ds(BASE, SX), :], local_sem.at[0])
    own.start()
    tables = [pltpu.make_async_copy(wp_hbm, wp, local_sem.at[1]), pltpu.make_async_copy(wh_hbm, wh, local_sem.at[2])]

    send_z = {-1: pl.ds(0, 4), 0: pl.ds(0, 16), 1: pl.ds(12, 4)}
    land_z = {-1: pl.ds(20, 4), 0: pl.ds(4, 16), 1: pl.ds(0, 4)}

    def plane_parts(dz, dx):
        if dx == 0:
            return x_ref.at[send_z[dz]], ext.at[land_z[dz], pl.ds(BASE, SX), :]
        if dx == -1:
            return xs_lo.at[send_z[dz]], xp.at[land_z[dz]]
        return xs_hi.at[send_z[dz]], xm.at[land_z[dz]]

    def across_parts(dz, dx, dy):
        src, dst_p, dst_x = (ys_lo, yp_hi, yx_hi) if dy == -1 else (ys_hi, yp_lo, yx_lo)
        if dx == 0:
            tiles = {-1: pl.ds(0, 1), 0: pl.ds(0, 4), 1: pl.ds(3, 1)}[dz]
            land = {-1: pl.ds(5, 1), 0: pl.ds(1, 4), 1: pl.ds(0, 1)}[dz]
            return src.at[tiles], dst_p.at[land]
        return src.at[pl.ds(4, 1)], dst_x.at[pl.ds((0 if dx == -1 else 3) + 1 - dz, 1)]

    plane_copies, across_copies = [], []
    for dz, dx in beside:
        src, dst = plane_parts(dz, dx)
        i = len(plane_copies)
        copy = pltpu.make_async_remote_copy(
            src_ref=src, dst_ref=dst, send_sem=send_sem.at[i], recv_sem=recv_sem.at[i],
            device_id=device(dz, dx, 0), device_id_type=MESH)
        plane_copies.append((copy, dst, dz, dx, 0))
    for dy in (-1, 1):
        for dz, dx in [(0, 0)] + beside:
            src, dst = across_parts(dz, dx, dy)
            i = 8 + len(across_copies)
            copy = pltpu.make_async_remote_copy(
                src_ref=src, dst_ref=dst, send_sem=send_sem.at[i], recv_sem=recv_sem.at[i],
                device_id=device(dz, dx, dy), device_id_type=MESH)
            across_copies.append((copy, dst, dz, dx, dy))

    back_copies = []
    for i, (dy, src, dst) in enumerate(((-1, ye_lo, yr_hi), (1, ye_hi, yr_lo))):
        copy = pltpu.make_async_remote_copy(
            src_ref=src, dst_ref=dst, send_sem=send_sem.at[26 + i], recv_sem=recv_sem.at[26 + i],
            device_id=device(0, 0, dy), device_id_type=MESH)
        back_copies.append((copy, dst, 0, 0, dy))

    lane = iota((128, 128), 1)
    low_half = iota((8, 128), 0) < 4

    def block(v, k):
        dz, dx = VARIANTS[v]
        if k < 6:
            return jnp.concatenate([ext[4 * k + j + dz, BASE + dx:BASE + 32 + dx, :] for j in range(4)], axis=0)
        pieces = []
        for j in range(16 if k == 6 else 8):
            zi = 16 * (k - 6) + j + dz
            pieces.append(jnp.where(low_half, ext[zi, BASE + 32 + dx:BASE + 40 + dx, :], ext[zi, BASE - 8 + dx:BASE + dx, :]))
        if k == 7:
            pieces.append(jnp.zeros((64, 128), F32))
        return jnp.concatenate(pieces, axis=0)

    def place(v, k):
        turned = (block(v, k) * SCALE).T
        if k == 7 and v > 4:
            turned = jnp.where(lane == 64 + v - 4, 1.0, turned)
        for c in range(8):
            shifted[v, k, pl.ds(8 + c, 16, stride=8), :] = turned[16 * c:16 * c + 16]
        return turned

    pl.semaphore_wait(barrier, n_plane - 1 + n_across * odd_side.astype(jnp.int32))

    @pl.when(odd_side)
    def _():
        for dy in (-1, 1):
            @pl.when(there(0, 0, dy))
            def _():
                pl.semaphore_signal(ready, inc=1, device_id=device(0, 0, dy), device_id_type=MESH)

    own.wait()
    for k in range(1, 5):
        turned = place(4, k)
        ys_lo[k - 1] = ye_lo[k] = turned[0:4]
        ys_hi[k - 1] = ye_hi[k] = turned[124:128]
    rim = jnp.concatenate([jnp.where(low_half, ext[4 + j, BASE:BASE + 8, :], ext[4 + j, BASE + 24:BASE + 32, :]) for j in range(SZ)], axis=0)
    turned = (rim * SCALE).T
    ys_lo[4] = turned[0:4]
    ys_hi[4] = turned[124:128]

    @pl.when(odd_side)
    def _():
        for copy, dst, dz, dx, dy in across_copies:
            pl.when(there(dz, dx, dy))(copy.start)

    xs_lo[...] = ext[4:20, BASE:BASE + 4, :]
    xs_hi[...] = ext[4:20, BASE + 28:BASE + 32, :]
    for copy, dst, dz, dx, dy in plane_copies:
        pl.when(there(dz, dx, 0))(copy.start)
    for copy in tables:
        copy.start()

    ext[0:24, 0:BASE] = jnp.zeros((24, BASE, 128), F32)
    ext[0:24, BASE + SX:PITCH] = jnp.zeros((24, PITCH - BASE - SX, 128), F32)
    ext[24:26] = jnp.zeros((2, PITCH, 128), F32)
    for copy, dst, dz, dx, dy in plane_copies + across_copies + back_copies:
        @pl.when(jnp.logical_not(there(-dz, -dx, -dy)))
        def _():
            dst[...] = jnp.zeros(dst.shape, F32)

    early = [(v, k) for v, ks in ((7, range(1, 4)), (1, range(2, 5))) for k in ks]
    for v, k in early:
        place(v, k)

    for copy in tables:
        copy.wait()
    row = iota((16, 256), 0)
    col = iota((16, 256), 1)
    row_dz = jnp.where(row >= 2, 1, 0)
    row_dx = jnp.where(row == 1, 1, jnp.where((row >= 2) & (row < 5), row - 3, 0))
    known = (row >= 1) & (row < 5)
    for half in range(2):
        vz = gz * SZ + 8 * half + col // 32
        vx = gx * SX + col % 32

        def outside(sign):
            z, x = vz + sign * row_dz, vx + sign * row_dx
            return (z < 0) | (z >= nz * SZ) | (x < 0) | (x >= nx * SX)

        wh[0, half, 192:208, :] = jnp.where(known & outside(1), MASKED, 0.0).astype(BF16)
        back = known & outside(-1)
        for g in range(1, 5):
            wh[g, half, 192:208, :] = jnp.where(back & (row == g), MASKED, 0.0).astype(BF16)

    for copy, dst, dz, dx, dy in plane_copies:
        pl.when(there(-dz, -dx, 0))(copy.wait_recv)
    ext[0:24, BASE + 32:BASE + 36, :] = xp[...]
    ext[0:24, BASE - 4:BASE, :] = xm[...]
    for v in (4, 5, 6, 7, 8, 0, 1, 2, 3):
        for k in (range(8) if v >= 4 else range(1, 5)):
            if (v, k) not in early and not (v == 4 and 1 <= k <= 4):
                turned = place(v, k)
                if v == 4:
                    ye_lo[k] = turned[0:4]
                    ye_hi[k] = turned[124:128]

    z_step = gz // 2

    def answer(at_step):
        @pl.when(jnp.logical_and(even, jnp.minimum(z_step, 3) == at_step))
        def _():
            pl.semaphore_wait(ready, n_beside)
            for copy, dst, dz, dx, dy in back_copies:
                pl.when(there(0, 0, dy))(copy.start)

    lane8 = iota((8, 128), 1)
    sub = iota((8, 128), 0)

    def turn(value, by, axis):
        by = by % value.shape[axis]
        return value if by == 0 else pltpu.roll(value, by, axis)

    for v in range(9):
        for k in (range(8) if v >= 4 else range(1, 5)):
            shifted[v, k, 0:8, :] = turn(shifted[v, k, 128:136, :], 1, 0)
            shifted[v, k, 136:144, :] = turn(shifted[v, k, 8:16, :], -1, 0)

    def steps(g):
        return (1,) if g == 0 else (-1, 0, 1)

    def offset_index(g, d):
        return 0 if g == 0 else 3 * g - 2 + d

    def build(g):
        v = g + 4
        for d, dy in enumerate(steps(g)):
            for k in range(8):
                lanes = slice(128 * k, 128 * k + 128)
                error = None
                for j in range(8):
                    diff = shifted[4, k, 8 + 16 * j:24 + 16 * j, :] - shifted[v, k, 8 + 16 * j + 8 * dy:24 + 16 * j + 8 * dy, :]
                    square = diff * diff
                    if error is not None:
                        square = square + error
                    rounded = square.astype(BF16)
                    lhs[g % 2, 128 * d + 16 * j:128 * d + 16 * j + 16, lanes] = rounded
                    error = square - rounded.astype(F32)

    def multiply(g):
        rows = 128 * len(steps(g))
        for w, table in enumerate((0, g)):
            if w == 1 and g == 0:
                continue
            for half in range(2):
                total = jnp.dot(lhs[g % 2, 0:rows, 256 * half:256 * half + 512], wp[table], preferred_element_type=F32)
                total = total + jnp.dot(lhs[g % 2, 0:rows, 768:1024], wh[table, half], preferred_element_type=F32)
                for part in range(2):
                    dist[g % 2, w, 2 * half + part, 0:rows, :] = total[:, 128 * part:128 * part + 128]

    low4 = sub < 4

    def weights(g, w, d, dy, n, first):
        cache = {}

        def get(t):
            if t not in cache:
                if 0 <= t < 16:
                    value = dist[g % 2, w, n, 128 * d + 8 * t:128 * d + 8 * t + 8, :]
                    if t == 15 and dy == 1:
                        value = jnp.where(sub == 7, 0.0, value)
                    elif t == 0 and dy == -1:
                        value = jnp.where(sub == 0, 0.0, value)
                    cache[t] = value
                elif t < 0:
                    cache[t] = jnp.where(sub == 0, 0.0, turn(get(16 + t), 1, 0))
                else:
                    cache[t] = jnp.where(sub == 7, 0.0, turn(get(t - 16), -1, 0))
            return cache[t]

        total = get(first - 3)
        for t in range(first - 2, first + 4):
            total = total + get(t)
        result = []
        for i in range(16):
            if i:
                total = total + (get(first + i + 3) - get(first + i - 4))
            if i < 4 or i >= 12:
                at = 8 * (i if i < 4 else i - 8)
                edge[offset_index(g, d), w if g else (1 if first else 0), n, at:at + 8, :] = total
            result.append(jnp.exp2(total))
        return result

    def gather(g):
        v = g + 4
        for n in range(4):
            lanes = slice(128 * n, 128 * n + 128)
            for d, dy in enumerate(steps(g)):
                ahead = weights(g, 0, d, dy, n, 0)
                behind = weights(g, 1 if g else 0, d, dy, n, -dy)
                for t in range(16):
                    rows = slice(8 * t, 8 * t + 8)
                    up = shifted[v, n + 1, 8 + 8 * (t + dy):16 + 8 * (t + dy), :]
                    down = shifted[8 - v, n + 1, 8 + 8 * (t - dy):16 + 8 * (t - dy), :]
                    part = ahead[t] * up + behind[t] * down
                    part_w = ahead[t] + behind[t]
                    if g == 0:
                        num[rows, lanes] = part
                        wsum[rows, lanes] = part_w
                    else:
                        num[rows, lanes] += part
                        wsum[rows, lanes] += part_w

    for g in range(5):
        for at_step, at_group in ((3, 0), (2, 2), (1, 2), (0, 3)):
            if g == at_group:
                answer(at_step)
        build(g)
        multiply(g)
        gather(g)

    for v in range(9):
        for n in range(4):
            low = shifted[v, n + 1, pl.ds(8, 8, stride=8), :]
            high = shifted[v, n + 1, pl.ds(8 + 71, 8, stride=8), :]
            edge_p[v, n, 0] = jnp.where(low4, turn(low, 1, 0), turn(high, 1, 0))
            edge_p[v, n, 1] = jnp.where(low4, low, high)
            edge_p[v, n, 2] = jnp.where(low4, turn(low, -1, 0), turn(high, -1, 0))

    @pl.when(even)
    def _():
        for copy, dst, dz, dx, dy in across_copies:
            pl.when(there(-dz, -dx, -dy))(copy.wait_recv)
        for k in range(6):
            rows_h[4, k] = jnp.concatenate([yp_lo[k], yp_hi[k]], axis=0)
        from_rim = []
        for j in range(3):
            lower = jnp.concatenate([yx_lo[j], yx_hi[j]], axis=0)
            upper = jnp.concatenate([yx_lo[3 + j], yx_hi[3 + j]], axis=0)
            from_rim.append(jnp.where(lane8 % 8 < 4, lower, upper))
        rows_h[4, 6] = turn(jnp.where(lane8 >= 96, from_rim[0], from_rim[1]), 32, 1)
        rows_h[4, 7] = jnp.where(lane8 < 64, turn(jnp.where(lane8 >= 96, from_rim[1], from_rim[2]), 32, 1), 0.0)

    @pl.when(odd_side)
    def _():
        for copy, dst, dz, dx, dy in back_copies:
            pl.when(there(0, 0, -dy))(copy.wait_recv)
        for k in range(8):
            rows_h[4, k] = jnp.concatenate([yr_lo[k], yr_hi[k]], axis=0)

    for dx in (-1, 1):
        v = 4 + dx
        for k in range(6):
            value = turn(rows_h[4, k], -dx, 1)
            edge_lane = 31 if dx == 1 else 0
            source = rows_h[4, 6 + k // 4]
            for j in range(4):
                src_lane = (4 * (k % 4) + j) * 8 + (0 if dx == 1 else 7)
                dst_lane = 32 * j + edge_lane
                value = jnp.where(lane8 == dst_lane, turn(source, dst_lane - src_lane, 1), value)
            rows_h[v, k] = value
        for m in range(2):
            value = turn(rows_h[4, 6 + m], -dx, 1)
            for zz in range(16 if m == 0 else 8):
                k = 4 * m + zz // 4
                src_lane = 32 * (zz % 4) + (0 if dx == 1 else 31)
                dst_lane = 8 * zz + (7 if dx == 1 else 0)
                value = jnp.where(lane8 == dst_lane, turn(rows_h[4, k], dst_lane - src_lane, 1), value)
            rows_h[v, 6 + m] = value
    for dx in (-1, 0, 1):
        for k in range(6):
            here = turn(rows_h[4 + dx, k], -32, 1)
            after = turn(rows_h[4 + dx, k + 1], -32, 1) if k < 5 else here
            rows_h[7 + dx, k] = jnp.where(lane8 < 96, here, after)
            if 1 <= k <= 4:
                here = turn(rows_h[4 + dx, k], 32, 1)
                before = turn(rows_h[4 + dx, k - 1], 32, 1)
                rows_h[1 + dx, k] = jnp.where(lane8 >= 32, here, before)
        here, after = turn(rows_h[4 + dx, 6], -8, 1), turn(rows_h[4 + dx, 7], -8, 1)
        rows_h[7 + dx, 6] = jnp.where(lane8 < 120, here, after)
        rows_h[7 + dx, 7] = after
    for v in range(5, 9):
        rows_h[v, 7] = jnp.where(lane8 >= 64, jnp.where(lane8 == 64 + v - 4, 1.0, 0.0), rows_h[v, 7])

    for k in range(8):
        lanes = slice(128 * k, 128 * k + 128)

        def inner_low(v):
            first = turn(shifted[v, k, 8:16, :], 3, 0)
            return jnp.where(low4, jnp.where(sub == 3, first, turn(rows_h[v, k], -1, 0)), rows_h[v, k])

        def inner_high(v):
            last = turn(shifted[v, k, 128:136, :], -3, 0)
            return jnp.where(low4, rows_h[v, k], jnp.where(sub == 4, last, turn(rows_h[v, k], 1, 0)))

        base, base_low, base_high = rows_h[4, k], inner_low(4), inner_high(4)
        for g in range(5):
            v = g + 4
            if g:
                moved, moved_low, moved_high = rows_h[v, k], inner_low(v), inner_high(v)
            else:
                moved, moved_low, moved_high = base, base_low, base_high
            for d, dy in enumerate(steps(g)):
                if dy == 0:
                    diff = base - moved
                elif dy == 1:
                    diff = base_high - moved_low
                else:
                    diff = base_low - moved_high
                square = diff * diff
                high = square.astype(BF16).astype(F32)
                i = offset_index(g, d)
                lhs_h[16 * i:16 * i + 16, lanes] = jnp.concatenate([high, square - high], axis=0).astype(BF16)

    for g in range(5):
        first, rows = (0, 208) if g == 0 else (16 * offset_index(g, 0), 48)
        for half in range(2):
            total = jnp.dot(lhs_h[first:first + rows, 256 * half:256 * half + 512], wp[g], preferred_element_type=F32)
            total = total + jnp.dot(lhs_h[first:first + rows, 768:1024], wh[g, half], preferred_element_type=F32)
            for part in range(2):
                dist_h[1 if g else 0, 2 * half + part, first:first + rows, :] = total[:, 128 * part:128 * part + 128]

    keep_lo = jnp.where((sub == 0) & (gy == 0), 0.0, 1.0)
    keep_hi = jnp.where((sub == 7) & (gy == ny - 1), 0.0, 1.0)

    def edge_weights(i, w, dy, n, w_at):
        x = dist_h[w, n, 16 * i:16 * i + 8, :] + dist_h[w, n, 16 * i + 8:16 * i + 16, :]
        inward = jnp.where((sub == 3) | (sub == 4), 0.0, jnp.where(low4, turn(x, -1, 0), turn(x, 1, 0)))
        x = x + inward
        inward = jnp.where((sub >= 2) & (sub < 6), 0.0, jnp.where(low4, turn(x, -2, 0), turn(x, 2, 0)))
        x = x + inward
        fewer = jnp.where((sub == 3) | (sub == 4), 0.0, jnp.where(low4, turn(x, -1, 0), turn(x, 1, 0)))
        if dy == 0:
            halo = fewer
        elif (dy == 1) == (w_at == 0):
            halo = jnp.where(low4, fewer, x)
        else:
            halo = jnp.where(low4, x, fewer)
        low = edge[i, w_at, n, pl.ds(0, 4, stride=8), :]
        high = edge[i, w_at, n, pl.ds(39, 4, stride=8), :]
        return jnp.exp2(jnp.concatenate([low, high], axis=0) + halo)

    for n in range(4):
        def partner(v, dy):
            value = edge_p[v, n, 1 + dy]
            if dy == 1:
                return jnp.where(sub == 7, turn(rows_h[v, n + 1], 3, 0), value)
            if dy == -1:
                return jnp.where(sub == 0, turn(rows_h[v, n + 1], -3, 0), value)
            return value

        total, total_w = edge_p[4, n, 1], jnp.ones((8, 128), F32)
        for g in range(5):
            for d, dy in enumerate(steps(g)):
                i = offset_index(g, d)
                ahead = edge_weights(i, 0, dy, n, 0)
                behind = edge_weights(i, 1 if g else 0, dy, n, 1)
                if dy == 1:
                    ahead, behind = ahead * keep_hi, behind * keep_lo
                elif dy == -1:
                    ahead, behind = ahead * keep_lo, behind * keep_hi
                total = total + (ahead * partner(g + 4, dy) + behind * partner(4 - g, -dy))
                total_w = total_w + (ahead + behind)
        rim_rows = total * (1.0 / SCALE) / total_w

        lanes = slice(128 * n, 128 * n + 128)
        top = shifted[4, n + 1, 8:136, :] + num[:, lanes]
        ordered[n] = top * (1.0 / SCALE) / (1.0 + wsum[:, lanes])
        pieces = [ordered[n, pl.ds(c, 16, stride=8), :] for c in range(8)]
        pieces = [jnp.where(low4, rim_rows, pieces[0][0:8]), pieces[0][8:16]] + pieces[1:7] + [
            pieces[7][0:8], jnp.where(low4, pieces[7][8:16], rim_rows)]
        out_ref[4 * n:4 * n + 4] = jnp.concatenate(pieces, axis=0).T.reshape(4, 32, 128)

    for copy, dst, dz, dx, dy in plane_copies:
        pl.when(there(dz, dx, dy))(copy.wait_send)
    for side, sent in ((odd_side, across_copies), (even, back_copies)):
        for copy, dst, dz, dx, dy in sent:
            pl.when(jnp.logical_and(side, there(dz, dx, dy)))(copy.wait_send)


def shards(planes, rims, noisy):
    def vmem(*shape, dtype=F32):
        return pltpu.VMEM(shape, dtype)

    return pl.pallas_call(
        kernel,
        out_shape=jax.ShapeDtypeStruct(noisy.shape, F32),
        in_specs=[pl.BlockSpec(memory_space=pl.ANY)] * 3,
        out_specs=pl.BlockSpec(memory_space=pltpu.VMEM),
        scratch_shapes=[
            vmem(26, PITCH, 128),
            vmem(16, 4, 128), vmem(16, 4, 128), vmem(24, 4, 128), vmem(24, 4, 128),
            vmem(5, 4, 128), vmem(5, 4, 128),
            vmem(6, 4, 128), vmem(6, 4, 128), vmem(6, 4, 128), vmem(6, 4, 128),
            vmem(8, 4, 128), vmem(8, 4, 128), vmem(8, 4, 128), vmem(8, 4, 128),
            vmem(9, 8, 144, 128),
            vmem(9, 8, 8, 128),
            vmem(5, 512, 256, dtype=BF16), vmem(5, 2, 256, 256, dtype=BF16),
            vmem(2, 384, 1024, dtype=BF16), vmem(2, 2, 4, 384, 128),
            vmem(128, 512), vmem(128, 512),
            vmem(208, 1024, dtype=BF16), vmem(2, 4, 208, 128),
            vmem(13, 2, 4, 64, 128), vmem(9, 4, 3, 8, 128),
            vmem(4, 128, 128),
            pltpu.SemaphoreType.DMA((3,)),
            pltpu.SemaphoreType.DMA((28,)),
            pltpu.SemaphoreType.DMA((28,)),
            pltpu.SemaphoreType.REGULAR,
        ],
        compiler_params=pltpu.CompilerParams(collective_id=0, has_side_effects=True, vmem_limit_bytes=54848 << 10),
    )(noisy, jnp.asarray(planes), jnp.asarray(rims))


def solution(mesh):
    planes, rims = box_tables()
    placed = P("gz", "gx", "gy")
    return jax.shard_map(
        functools.partial(shards, planes, rims), mesh=mesh, in_specs=(placed,), out_specs=placed, check_vma=False
    )
```

time: 23.6 us -> 16.9 us (0.72)
  the two profiles are of different devices: /device:TPU:1 before, /device:TPU:224 now
where the time goes in v2:
time: 16.9 us; the launch traced here: 16.8 us
  Pallas kernels  16.1 us (95%)
  local copies, waits for them, and re-layouts  0.71 us (4%)
    pallas_call x1, Pallas kernels, shards(): pl.pallas_call(kernel, out_shape=jax.ShapeDtypeStruct(noisy.shape, F32),...  16.1 us
    unnamed x1, local copies, waits for them, and re-layouts  0.71 us

profile of v2, /device:TPU:224, one launch (start us, length us, event | category | flops | bytes accessed | tf_op | source)
XLA Modules:
  0.0 16.8 jit_solution(13083317981112044396)
XLA Ops:
  0.0 16.1 %shard_map.37 = f32[16,32,128]{2,1,0:T(8,128)S(1)} custom-call(f32[16,32,128]{2,1,0:T(8,128)} %x_ref.1, bf16[5,512,256]{2,1,0:T(8,128)(2,1)} %constant.4.clone.wp_hbm, bf16[5,2,256,256]{3,2,1,0:T(8,128)(2,1)} %constant.5.clone.wh_hbm), custom_call_target="tpu_custom_call" | custom-call | tf_op jit(solution)/shard_map/pallas_call | solution.py:507
  16.1 0.7 %copy.5 = f32[16,32,128]{2,1,0:T(8,128)} copy(f32[16,32,128]{2,1,0:T(8,128)S(1)} %shard_map.37) | data formatting | bytes 524288

commit v3 on v2

--- a/solution.py
+++ b/solution.py
@@ -16,37 +16,36 @@
 SZ, SX, SY = 16, 32, 128
 BASE, PITCH = 16, 64
 MASKED = -1000.0
+ANSWER_AT = 2
 MESH = pl.DeviceIdType.MESH
 F32, BF16 = jnp.float32, jnp.bfloat16
 
 
 def box_tables():
     n = np.arange(256)
-    k = np.arange(512)
-    j = np.arange(256)
-    zk, xk = k // 32, k % 32
-    zj, s = j // 8, j % 8
-    xj = np.where(s < 4, 32 + s, s - 8)
-    planes, rims = [], []
+    lane = np.arange(1024)
+    rim = (lane < 128) | (lane >= 896)
+    k, s = lane - 128, lane % 8
+    zl = np.where(rim, lane % 128 // 8 + np.where(lane < 128, 0, 8), k // 32)
+    xl = np.where(rim, np.where(s < 4, 32 + s, s - 8), k % 32)
+    real = ~(rim & (lane % 128 >= 120))
+    tables = []
     for dz, dx in GROUPS:
-        xc = n % 32 - dx
-        zc = 4 + n // 32 - dz
-        near = (abs(zk[:, None] - zc) <= 3) & (abs(xk[:, None] - xc) <= 3)
-        planes.append(-near.astype(np.float32))
         halves = []
         for half in range(2):
-            near = (abs(zj[:, None] - zc - 8 * half) <= 3) & (abs(xj[:, None] - xc) <= 3) & (j < 192)[:, None]
-            halves.append(-near.astype(np.float32))
-        rims.append(np.stack(halves))
-    return np.stack(planes).astype(ml_dtypes.bfloat16), np.stack(rims).astype(ml_dtypes.bfloat16)
+            near = (abs(zl[:, None] - (4 + 8 * half + n // 32 - dz)) <= 3) & (abs(xl[:, None] - (n % 32 - dx)) <= 3)
+            near = near & real[:, None]
+            halves.append(-near[384 * half:384 * half + 640].astype(np.float32))
+        tables.append(np.stack(halves))
+    return np.stack(tables).astype(ml_dtypes.bfloat16)
 
 
 def iota(shape, dim):
     return lax.broadcasted_iota(jnp.int32, shape, dim)
 
 
-def kernel(x_ref, wp_hbm, wh_hbm, out_ref, ext, xs_lo, xs_hi, xp, xm, ys_lo, ys_hi, yp_lo, yp_hi, yx_lo, yx_hi,
-           ye_lo, ye_hi, yr_lo, yr_hi, shifted, rows_h, wp, wh, lhs, dist, num, wsum, lhs_h, dist_h, edge, edge_p, ordered, local_sem, send_sem, recv_sem, ready):
+def kernel(x_ref, box_hbm, out_ref, ext, xs_lo, xs_hi, xp, xm, ys_lo, ys_hi, yp_lo, yp_hi, yx_lo, yx_hi, ye_lo, ye_hi, yr_lo, yr_hi,
+           shifted, rows_h, box, lhs, dist, num, wsum, lhs_h, dist_h, edge, edge_p, ordered, local_sem, send_sem, recv_sem, ready):
     gx, gy, gz = lax.axis_index("gx"), lax.axis_index("gy"), lax.axis_index("gz")
     nx, ny, nz = lax.axis_size("gx"), lax.axis_size("gy"), lax.axis_size("gz")
     even = gy % 2 == 0
@@ -66,9 +65,14 @@
     around = [(dz, dx) for dz in (-1, 0, 1) for dx in (-1, 0, 1)]
     beside = [o for o in around if o != (0, 0)]
     barrier = pltpu.get_barrier_semaphore()
+    direct_to = nz
     for dy in (-1, 1):
         for dz, dx in around:
-            @pl.when(jnp.logical_and(even, there(dz, dx, dy)))
+            greets = jnp.logical_and(even, there(dz, dx, dy))
+            if (dz, dx) != (0, 0):
+                greets = jnp.logical_and(greets, gz < direct_to)
+
+            @pl.when(greets)
             def _():
                 pl.semaphore_signal(barrier, inc=1, device_id=device(dz, dx, dy), device_id_type=MESH)
     for dz, dx in beside:
@@ -81,18 +85,19 @@
 
     n_plane = (1 + count(gz, nz)) * (1 + count(gx, nx))
     n_beside = count(gy, ny)
-    n_across = n_plane * n_beside
+    n_direct = sum(((gz + dz >= 0) & (gz + dz < direct_to)).astype(jnp.int32) for dz in (-1, 0, 1))
+    n_across = n_beside * (n_direct * (1 + count(gx, nx)) + (gz >= direct_to).astype(jnp.int32))
 
     own = pltpu.make_async_copy(x_ref, ext.at[pl.ds(4, SZ), pl.ds(BASE, SX), :], local_sem.at[0])
     own.start()
-    tables = [pltpu.make_async_copy(wp_hbm, wp, local_sem.at[1]), pltpu.make_async_copy(wh_hbm, wh, local_sem.at[2])]
+    tables = [pltpu.make_async_copy(box_hbm, box, local_sem.at[1])]
 
     send_z = {-1: pl.ds(0, 4), 0: pl.ds(0, 16), 1: pl.ds(12, 4)}
     land_z = {-1: pl.ds(20, 4), 0: pl.ds(4, 16), 1: pl.ds(0, 4)}
 
     def plane_parts(dz, dx):
         if dx == 0:
-            return x_ref.at[send_z[dz]], ext.at[land_z[dz], pl.ds(BASE, SX), :]
+            return ext.at[pl.ds(4 + send_z[dz].start, 4), pl.ds(BASE, SX), :], ext.at[land_z[dz], pl.ds(BASE, SX), :]
         if dx == -1:
             return xs_lo.at[send_z[dz]], xp.at[land_z[dz]]
         return xs_hi.at[send_z[dz]], xm.at[land_z[dz]]
@@ -114,20 +119,19 @@
             device_id=device(dz, dx, 0), device_id_type=MESH)
         plane_copies.append((copy, dst, dz, dx, 0))
     for dy in (-1, 1):
-        for dz, dx in [(0, 0)] + beside:
+        for dz, dx in sorted(around, key=lambda o: -abs(o[0]) - abs(o[1])):
             src, dst = across_parts(dz, dx, dy)
-            i = 8 + len(across_copies)
+            i = 10 + len(across_copies)
             copy = pltpu.make_async_remote_copy(
                 src_ref=src, dst_ref=dst, send_sem=send_sem.at[i], recv_sem=recv_sem.at[i],
                 device_id=device(dz, dx, dy), device_id_type=MESH)
             across_copies.append((copy, dst, dz, dx, dy))
-
-    back_copies = []
+    row_copies = []
     for i, (dy, src, dst) in enumerate(((-1, ye_lo, yr_hi), (1, ye_hi, yr_lo))):
         copy = pltpu.make_async_remote_copy(
-            src_ref=src, dst_ref=dst, send_sem=send_sem.at[26 + i], recv_sem=recv_sem.at[26 + i],
+            src_ref=src, dst_ref=dst, send_sem=send_sem.at[8 + i], recv_sem=recv_sem.at[8 + i],
             device_id=device(0, 0, dy), device_id_type=MESH)
-        back_copies.append((copy, dst, 0, 0, dy))
+        row_copies.append((copy, dst, 0, 0, dy))
 
     lane = iota((128, 128), 1)
     low_half = iota((8, 128), 0) < 4
@@ -137,20 +141,19 @@
         if k < 6:
             return jnp.concatenate([ext[4 * k + j + dz, BASE + dx:BASE + 32 + dx, :] for j in range(4)], axis=0)
         pieces = []
-        for j in range(16 if k == 6 else 8):
-            zi = 16 * (k - 6) + j + dz
+        for j in range(16):
+            zi = 8 * (k - 6) + j + dz
             pieces.append(jnp.where(low_half, ext[zi, BASE + 32 + dx:BASE + 40 + dx, :], ext[zi, BASE - 8 + dx:BASE + dx, :]))
-        if k == 7:
-            pieces.append(jnp.zeros((64, 128), F32))
         return jnp.concatenate(pieces, axis=0)
 
     def place(v, k):
-        turned = (block(v, k) * SCALE).T
-        if k == 7 and v > 4:
-            turned = jnp.where(lane == 64 + v - 4, 1.0, turned)
+        whole = turned = (block(v, k) * SCALE).T
+        if k >= 6:
+            mark = jnp.where(lane == 120 + v - 4, 1.0, 0.0) if v > 4 else 0.0
+            turned = jnp.where(lane >= 120, mark, turned)
         for c in range(8):
             shifted[v, k, pl.ds(8 + c, 16, stride=8), :] = turned[16 * c:16 * c + 16]
-        return turned
+        return whole
 
     pl.semaphore_wait(barrier, n_plane - 1 + n_across * odd_side.astype(jnp.int32))
 
@@ -162,19 +165,27 @@
                 pl.semaphore_signal(ready, inc=1, device_id=device(0, 0, dy), device_id_type=MESH)
 
     own.wait()
+    def place_and_keep(v, k):
+        turned = place(v, k)
+        if v == 4:
+            ye_lo[k] = turned[0:4]
+            ye_hi[k] = turned[124:128]
+            if 1 <= k <= 4:
+                ys_lo[k - 1] = turned[0:4]
+                ys_hi[k - 1] = turned[124:128]
+
     for k in range(1, 5):
-        turned = place(4, k)
-        ys_lo[k - 1] = ye_lo[k] = turned[0:4]
-        ys_hi[k - 1] = ye_hi[k] = turned[124:128]
+        place_and_keep(4, k)
     rim = jnp.concatenate([jnp.where(low_half, ext[4 + j, BASE:BASE + 8, :], ext[4 + j, BASE + 24:BASE + 32, :]) for j in range(SZ)], axis=0)
     turned = (rim * SCALE).T
     ys_lo[4] = turned[0:4]
     ys_hi[4] = turned[124:128]
 
-    @pl.when(odd_side)
-    def _():
-        for copy, dst, dz, dx, dy in across_copies:
-            pl.when(there(dz, dx, dy))(copy.start)
+    def across_sent(dz, dx, dy):
+        return jnp.logical_and(jnp.logical_and(odd_side, gz + dz < direct_to), there(dz, dx, dy))
+
+    for copy, dst, dz, dx, dy in across_copies:
+        pl.when(across_sent(dz, dx, dy))(copy.start)
 
     xs_lo[...] = ext[4:20, BASE:BASE + 4, :]
     xs_hi[...] = ext[4:20, BASE + 28:BASE + 32, :]
@@ -186,7 +197,7 @@
     ext[0:24, 0:BASE] = jnp.zeros((24, BASE, 128), F32)
     ext[0:24, BASE + SX:PITCH] = jnp.zeros((24, PITCH - BASE - SX, 128), F32)
     ext[24:26] = jnp.zeros((2, PITCH, 128), F32)
-    for copy, dst, dz, dx, dy in plane_copies + across_copies + back_copies:
+    for copy, dst, dz, dx, dy in plane_copies + row_copies + across_copies:
         @pl.when(jnp.logical_not(there(-dz, -dx, -dy)))
         def _():
             dst[...] = jnp.zeros(dst.shape, F32)
@@ -197,7 +208,7 @@
 
     for copy in tables:
         copy.wait()
-    row = iota((16, 256), 0)
+    row = iota((16, 256), 0) - 8
     col = iota((16, 256), 1)
     row_dz = jnp.where(row >= 2, 1, 0)
     row_dx = jnp.where(row == 1, 1, jnp.where((row >= 2) & (row < 5), row - 3, 0))
@@ -210,31 +221,35 @@
             z, x = vz + sign * row_dz, vx + sign * row_dx
             return (z < 0) | (z >= nz * SZ) | (x < 0) | (x >= nx * SX)
 
-        wh[0, half, 192:208, :] = jnp.where(known & outside(1), MASKED, 0.0).astype(BF16)
+        mask_rows = slice(112 + 512 * half, 128 + 512 * half)
+        box[0, half, mask_rows, :] = jnp.where(known & outside(1), MASKED, box[0, half, mask_rows, :].astype(F32)).astype(BF16)
         back = known & outside(-1)
         for g in range(1, 5):
-            wh[g, half, 192:208, :] = jnp.where(back & (row == g), MASKED, 0.0).astype(BF16)
+            box[g, half, mask_rows, :] = jnp.where(back & (row == g), MASKED, box[g, half, mask_rows, :].astype(F32)).astype(BF16)
 
     for copy, dst, dz, dx, dy in plane_copies:
         pl.when(there(-dz, -dx, 0))(copy.wait_recv)
     ext[0:24, BASE + 32:BASE + 36, :] = xp[...]
     ext[0:24, BASE - 4:BASE, :] = xm[...]
-    for v in (4, 5, 6, 7, 8, 0, 1, 2, 3):
-        for k in (range(8) if v >= 4 else range(1, 5)):
-            if (v, k) not in early and not (v == 4 and 1 <= k <= 4):
-                turned = place(v, k)
-                if v == 4:
-                    ye_lo[k] = turned[0:4]
-                    ye_hi[k] = turned[124:128]
-
-    z_step = gz // 2
-
-    def answer(at_step):
-        @pl.when(jnp.logical_and(even, jnp.minimum(z_step, 3) == at_step))
+    for k in range(8):
+        if k < 1 or k > 4:
+            place_and_keep(4, k)
+
+    def send_rows():
+        for copy, dst, dz, dx, dy in row_copies:
+            pl.when(there(0, 0, dy))(copy.start)
+
+    pl.when(jnp.logical_and(odd_side, gz >= direct_to))(send_rows)
+    for v in (5, 6, 7, 8, 0, 1, 2, 3):
+        for k in (range(8) if v > 4 else range(1, 5)):
+            if (v, k) not in early:
+                place(v, k)
+
+    def answer():
+        @pl.when(even)
         def _():
             pl.semaphore_wait(ready, n_beside)
-            for copy, dst, dz, dx, dy in back_copies:
-                pl.when(there(0, 0, dy))(copy.start)
+            send_rows()
 
     lane8 = iota((8, 128), 1)
     sub = iota((8, 128), 0)
@@ -254,11 +269,15 @@
     def offset_index(g, d):
         return 0 if g == 0 else 3 * g - 2 + d
 
-    def build(g):
+    def at_lanes(k):
+        tile = k + 1 if k < 6 else 7 * (k - 6)
+        return slice(128 * tile, 128 * tile + 128)
+
+    def build(g, ks):
         v = g + 4
         for d, dy in enumerate(steps(g)):
-            for k in range(8):
-                lanes = slice(128 * k, 128 * k + 128)
+            for k in ks:
+                lanes = at_lanes(k)
                 error = None
                 for j in range(8):
                     diff = shifted[4, k, 8 + 16 * j:24 + 16 * j, :] - shifted[v, k, 8 + 16 * j + 8 * dy:24 + 16 * j + 8 * dy, :]
@@ -269,16 +288,14 @@
                     lhs[g % 2, 128 * d + 16 * j:128 * d + 16 * j + 16, lanes] = rounded
                     error = square - rounded.astype(F32)
 
-    def multiply(g):
+    def multiply(g, piece):
         rows = 128 * len(steps(g))
-        for w, table in enumerate((0, g)):
-            if w == 1 and g == 0:
-                continue
-            for half in range(2):
-                total = jnp.dot(lhs[g % 2, 0:rows, 256 * half:256 * half + 512], wp[table], preferred_element_type=F32)
-                total = total + jnp.dot(lhs[g % 2, 0:rows, 768:1024], wh[table, half], preferred_element_type=F32)
-                for part in range(2):
-                    dist[g % 2, w, 2 * half + part, 0:rows, :] = total[:, 128 * part:128 * part + 128]
+        half, w = piece // 2, piece % 2
+        if w == 0 or g:
+            table = g if w else 0
+            total = jnp.dot(lhs[g % 2, 0:rows, 384 * half:384 * half + 640], box[table, half], preferred_element_type=F32)
+            for part in range(2):
+                dist[g % 2, w, 2 * half + part, 0:rows, :] = total[:, 128 * part:128 * part + 128]
 
     low4 = sub < 4
 
@@ -313,9 +330,9 @@
             result.append(jnp.exp2(total))
         return result
 
-    def gather(g):
+    def gather(g, ns):
         v = g + 4
-        for n in range(4):
+        for n in ns:
             lanes = slice(128 * n, 128 * n + 128)
             for d, dy in enumerate(steps(g)):
                 ahead = weights(g, 0, d, dy, n, 0)
@@ -333,13 +350,17 @@
                         num[rows, lanes] += part
                         wsum[rows, lanes] += part_w
 
-    for g in range(5):
-        for at_step, at_group in ((3, 0), (2, 2), (1, 2), (0, 3)):
-            if g == at_group:
-                answer(at_step)
-        build(g)
-        multiply(g)
-        gather(g)
+    build(0, range(8))
+    for g in range(6):
+        if g == ANSWER_AT:
+            answer()
+        for piece in range(4):
+            if g < 5:
+                multiply(g, piece)
+            if g < 4:
+                build(g + 1, (2 * piece, 2 * piece + 1))
+            if g > 0:
+                gather(g - 1, (piece,))
 
     for v in range(9):
         for n in range(4):
@@ -349,7 +370,9 @@
             edge_p[v, n, 1] = jnp.where(low4, low, high)
             edge_p[v, n, 2] = jnp.where(low4, turn(low, -1, 0), turn(high, -1, 0))
 
-    @pl.when(even)
+    got_across = jnp.logical_and(even, gz < direct_to)
+
+    @pl.when(got_across)
     def _():
         for copy, dst, dz, dx, dy in across_copies:
             pl.when(there(-dz, -dx, -dy))(copy.wait_recv)
@@ -361,11 +384,11 @@
             upper = jnp.concatenate([yx_lo[3 + j], yx_hi[3 + j]], axis=0)
             from_rim.append(jnp.where(lane8 % 8 < 4, lower, upper))
         rows_h[4, 6] = turn(jnp.where(lane8 >= 96, from_rim[0], from_rim[1]), 32, 1)
-        rows_h[4, 7] = jnp.where(lane8 < 64, turn(jnp.where(lane8 >= 96, from_rim[1], from_rim[2]), 32, 1), 0.0)
-
-    @pl.when(odd_side)
+        rows_h[4, 7] = turn(jnp.where(lane8 >= 32, from_rim[1], from_rim[2]), -32, 1)
+
+    @pl.when(jnp.logical_not(got_across))
     def _():
-        for copy, dst, dz, dx, dy in back_copies:
+        for copy, dst, dz, dx, dy in row_copies:
             pl.when(there(0, 0, -dy))(copy.wait_recv)
         for k in range(8):
             rows_h[4, k] = jnp.concatenate([yr_lo[k], yr_hi[k]], axis=0)
@@ -376,15 +399,16 @@
             value = turn(rows_h[4, k], -dx, 1)
             edge_lane = 31 if dx == 1 else 0
             source = rows_h[4, 6 + k // 4]
+            first_z = 4 * k - 8 * (k // 4)
             for j in range(4):
-                src_lane = (4 * (k % 4) + j) * 8 + (0 if dx == 1 else 7)
+                src_lane = (first_z + j) * 8 + (0 if dx == 1 else 7)
                 dst_lane = 32 * j + edge_lane
                 value = jnp.where(lane8 == dst_lane, turn(source, dst_lane - src_lane, 1), value)
             rows_h[v, k] = value
         for m in range(2):
             value = turn(rows_h[4, 6 + m], -dx, 1)
-            for zz in range(16 if m == 0 else 8):
-                k = 4 * m + zz // 4
+            for zz in range(16):
+                k = 2 * m + zz // 4
                 src_lane = 32 * (zz % 4) + (0 if dx == 1 else 31)
                 dst_lane = 8 * zz + (7 if dx == 1 else 0)
                 value = jnp.where(lane8 == dst_lane, turn(rows_h[4, k], dst_lane - src_lane, 1), value)
@@ -398,14 +422,15 @@
                 here = turn(rows_h[4 + dx, k], 32, 1)
                 before = turn(rows_h[4 + dx, k - 1], 32, 1)
                 rows_h[1 + dx, k] = jnp.where(lane8 >= 32, here, before)
-        here, after = turn(rows_h[4 + dx, 6], -8, 1), turn(rows_h[4 + dx, 7], -8, 1)
-        rows_h[7 + dx, 6] = jnp.where(lane8 < 120, here, after)
-        rows_h[7 + dx, 7] = after
-    for v in range(5, 9):
-        rows_h[v, 7] = jnp.where(lane8 >= 64, jnp.where(lane8 == 64 + v - 4, 1.0, 0.0), rows_h[v, 7])
+        for m in range(2):
+            rows_h[7 + dx, 6 + m] = turn(rows_h[4 + dx, 6 + m], -8, 1)
+    for v in range(4, 9):
+        mark = jnp.where(lane8 == 120 + v - 4, 1.0, 0.0) if v > 4 else 0.0
+        for m in range(2):
+            rows_h[v, 6 + m] = jnp.where(lane8 >= 120, mark, rows_h[v, 6 + m])
 
     for k in range(8):
-        lanes = slice(128 * k, 128 * k + 128)
+        lanes = at_lanes(k)
 
         def inner_low(v):
             first = turn(shifted[v, k, 8:16, :], 3, 0)
@@ -437,8 +462,7 @@
     for g in range(5):
         first, rows = (0, 208) if g == 0 else (16 * offset_index(g, 0), 48)
         for half in range(2):
-            total = jnp.dot(lhs_h[first:first + rows, 256 * half:256 * half + 512], wp[g], preferred_element_type=F32)
-            total = total + jnp.dot(lhs_h[first:first + rows, 768:1024], wh[g, half], preferred_element_type=F32)
+            total = jnp.dot(lhs_h[first:first + rows, 384 * half:384 * half + 640], box[g, half], preferred_element_type=F32)
             for part in range(2):
                 dist_h[1 if g else 0, 2 * half + part, first:first + rows, :] = total[:, 128 * part:128 * part + 128]
 
@@ -495,19 +519,20 @@
 
     for copy, dst, dz, dx, dy in plane_copies:
         pl.when(there(dz, dx, dy))(copy.wait_send)
-    for side, sent in ((odd_side, across_copies), (even, back_copies)):
-        for copy, dst, dz, dx, dy in sent:
-            pl.when(jnp.logical_and(side, there(dz, dx, dy)))(copy.wait_send)
-
-
-def shards(planes, rims, noisy):
+    for copy, dst, dz, dx, dy in across_copies:
+        pl.when(across_sent(dz, dx, dy))(copy.wait_send)
+    for copy, dst, dz, dx, dy in row_copies:
+        pl.when(jnp.logical_and(there(dz, dx, dy), jnp.logical_or(even, gz >= direct_to)))(copy.wait_send)
+
+
+def shards(tables, noisy):
     def vmem(*shape, dtype=F32):
         return pltpu.VMEM(shape, dtype)
 
     return pl.pallas_call(
         kernel,
         out_shape=jax.ShapeDtypeStruct(noisy.shape, F32),
-        in_specs=[pl.BlockSpec(memory_space=pl.ANY)] * 3,
+        in_specs=[pl.BlockSpec(memory_space=pl.ANY)] * 2,
         out_specs=pl.BlockSpec(memory_space=pltpu.VMEM),
         scratch_shapes=[
             vmem(26, PITCH, 128),
@@ -517,24 +542,23 @@
             vmem(8, 4, 128), vmem(8, 4, 128), vmem(8, 4, 128), vmem(8, 4, 128),
             vmem(9, 8, 144, 128),
             vmem(9, 8, 8, 128),
-            vmem(5, 512, 256, dtype=BF16), vmem(5, 2, 256, 256, dtype=BF16),
+            vmem(5, 2, 640, 256, dtype=BF16),
             vmem(2, 384, 1024, dtype=BF16), vmem(2, 2, 4, 384, 128),
             vmem(128, 512), vmem(128, 512),
             vmem(208, 1024, dtype=BF16), vmem(2, 4, 208, 128),
             vmem(13, 2, 4, 64, 128), vmem(9, 4, 3, 8, 128),
             vmem(4, 128, 128),
-            pltpu.SemaphoreType.DMA((3,)),
+            pltpu.SemaphoreType.DMA((2,)),
             pltpu.SemaphoreType.DMA((28,)),
             pltpu.SemaphoreType.DMA((28,)),
             pltpu.SemaphoreType.REGULAR,
         ],
         compiler_params=pltpu.CompilerParams(collective_id=0, has_side_effects=True, vmem_limit_bytes=54848 << 10),
-    )(noisy, jnp.asarray(planes), jnp.asarray(rims))
+    )(noisy, jnp.asarray(tables))
 
 
 def solution(mesh):
-    planes, rims = box_tables()
     placed = P("gz", "gx", "gy")
     return jax.shard_map(
-        functools.partial(shards, planes, rims), mesh=mesh, in_specs=(placed,), out_specs=placed, check_vma=False
+        functools.partial(shards, box_tables()), mesh=mesh, in_specs=(placed,), out_specs=placed, check_vma=False
     )

time: 16.9 us -> 16.2 us (0.959)
  the two profiles are of different devices: /device:TPU:224 before, /device:TPU:1 now
where the time goes in v3:
time: 16.2 us; the launch traced here: 16.1 us
  Pallas kernels  15.4 us (95%)
  local copies, waits for them, and re-layouts  0.71 us (4%)
    pallas_call x1, Pallas kernels, shards(): pl.pallas_call(kernel, out_shape=jax.ShapeDtypeStruct(noisy.shape, F32),...  15.4 us
    unnamed x1, local copies, waits for them, and re-layouts  0.71 us

profile of v3, /device:TPU:1, one launch (start us, length us, event | category | flops | bytes accessed | tf_op | source)
XLA Modules:
  0.0 16.1 jit_solution(11837964298729019561)
XLA Ops:
  0.0 15.4 %shard_map.28 = f32[16,32,128]{2,1,0:T(8,128)S(1)} custom-call(f32[16,32,128]{2,1,0:T(8,128)} %x_ref.1, bf16[5,2,640,256]{3,2,1,0:T(8,128)(2,1)} %constant.2.clone.box_hbm), custom_call_target="tpu_custom_call" | custom-call | tf_op jit(solution)/shard_map/pallas_call | solution.py:532
  15.4 0.7 %copy.4 = f32[16,32,128]{2,1,0:T(8,128)} copy(f32[16,32,128]{2,1,0:T(8,128)S(1)} %shard_map.28) | data formatting | bytes 524288

commit v4 on v3

--- a/solution.py
+++ b/solution.py
@@ -16,7 +16,8 @@
 SZ, SX, SY = 16, 32, 128
 BASE, PITCH = 16, 64
 MASKED = -1000.0
-ANSWER_AT = 2
+ANSWER_AT, ANSWER_LATE, LATE_BELOW = 2, 4, 2
+ROWS_FIRST_BELOW = 3
 MESH = pl.DeviceIdType.MESH
 F32, BF16 = jnp.float32, jnp.bfloat16
 
@@ -45,7 +46,7 @@
 
 
 def kernel(x_ref, box_hbm, out_ref, ext, xs_lo, xs_hi, xp, xm, ys_lo, ys_hi, yp_lo, yp_hi, yx_lo, yx_hi, ye_lo, ye_hi, yr_lo, yr_hi,
-           shifted, rows_h, box, lhs, dist, num, wsum, lhs_h, dist_h, edge, edge_p, ordered, local_sem, send_sem, recv_sem, ready):
+           shifted, rows_h, box, lhs, dist, num, wsum, lhs_h, dist_h, edge, edge_sum, edge_p, ordered, local_sem, send_sem, recv_sem, ready):
     gx, gy, gz = lax.axis_index("gx"), lax.axis_index("gy"), lax.axis_index("gz")
     nx, ny, nz = lax.axis_size("gx"), lax.axis_size("gy"), lax.axis_size("gz")
     even = gy % 2 == 0
@@ -65,7 +66,7 @@
     around = [(dz, dx) for dz in (-1, 0, 1) for dx in (-1, 0, 1)]
     beside = [o for o in around if o != (0, 0)]
     barrier = pltpu.get_barrier_semaphore()
-    direct_to = nz
+    direct_to = nz - 2
     for dy in (-1, 1):
         for dz, dx in around:
             greets = jnp.logical_and(even, there(dz, dx, dy))
@@ -165,6 +166,17 @@
                 pl.semaphore_signal(ready, inc=1, device_id=device(0, 0, dy), device_id_type=MESH)
 
     own.wait()
+    xs_lo[...] = ext[4:20, BASE:BASE + 4, :]
+    xs_hi[...] = ext[4:20, BASE + 28:BASE + 32, :]
+    rows_first = jnp.logical_and(odd_side, gz < ROWS_FIRST_BELOW)
+
+    def send_planes():
+        for copy, dst, dz, dx, dy in plane_copies:
+            pl.when(there(dz, dx, 0))(copy.start)
+
+    pl.when(jnp.logical_not(rows_first))(send_planes)
+    for copy in tables:
+        copy.start()
     def place_and_keep(v, k):
         turned = place(v, k)
         if v == 4:
@@ -187,13 +199,7 @@
     for copy, dst, dz, dx, dy in across_copies:
         pl.when(across_sent(dz, dx, dy))(copy.start)
 
-    xs_lo[...] = ext[4:20, BASE:BASE + 4, :]
-    xs_hi[...] = ext[4:20, BASE + 28:BASE + 32, :]
-    for copy, dst, dz, dx, dy in plane_copies:
-        pl.when(there(dz, dx, 0))(copy.start)
-    for copy in tables:
-        copy.start()
-
+    pl.when(rows_first)(send_planes)
     ext[0:24, 0:BASE] = jnp.zeros((24, BASE, 128), F32)
     ext[0:24, BASE + SX:PITCH] = jnp.zeros((24, PITCH - BASE - SX, 128), F32)
     ext[24:26] = jnp.zeros((2, PITCH, 128), F32)
@@ -245,8 +251,8 @@
             if (v, k) not in early:
                 place(v, k)
 
-    def answer():
-        @pl.when(even)
+    def answer(here):
+        @pl.when(jnp.logical_and(even, here))
         def _():
             pl.semaphore_wait(ready, n_beside)
             send_rows()
@@ -353,7 +359,9 @@
     build(0, range(8))
     for g in range(6):
         if g == ANSWER_AT:
-            answer()
+            answer(gz >= LATE_BELOW)
+        elif g == ANSWER_LATE:
+            answer(gz < LATE_BELOW)
         for piece in range(4):
             if g < 5:
                 multiply(g, piece)
@@ -369,6 +377,22 @@
             edge_p[v, n, 0] = jnp.where(low4, turn(low, 1, 0), turn(high, 1, 0))
             edge_p[v, n, 1] = jnp.where(low4, low, high)
             edge_p[v, n, 2] = jnp.where(low4, turn(low, -1, 0), turn(high, -1, 0))
+
+    for i in range(13):
+        for w in range(2):
+            for n in range(4):
+                low = edge[i, w, n, pl.ds(0, 4, stride=8), :]
+                high = edge[i, w, n, pl.ds(39, 4, stride=8), :]
+                edge_sum[i, w, n] = jnp.concatenate([low, high], axis=0)
+
+    for n in range(4):
+        lanes = slice(128 * n, 128 * n + 128)
+        top = shifted[4, n + 1, 8:136, :] + num[:, lanes]
+        ordered[n] = top * (1.0 / SCALE) / (1.0 + wsum[:, lanes])
+        pieces = [ordered[n, pl.ds(c, 16, stride=8), :] for c in range(8)]
+        out_ref[4 * n:4 * n + 4] = jnp.concatenate(pieces, axis=0).T.reshape(4, 32, 128)
+    column = iota((4, 32, 128), 2)
+    is_rim = (column < 4) | (column >= 124)
 
     got_across = jnp.logical_and(even, gz < direct_to)
 
@@ -407,7 +431,9 @@
             rows_h[v, k] = value
         for m in range(2):
             value = turn(rows_h[4, 6 + m], -dx, 1)
-            for zz in range(16):
+            if m == 1:
+                value = jnp.where(lane8 < 64, turn(rows_h[v, 6], 64, 1), value)
+            for zz in range(8 * m, 16):
                 k = 2 * m + zz // 4
                 src_lane = 32 * (zz % 4) + (0 if dx == 1 else 31)
                 dst_lane = 8 * zz + (7 if dx == 1 else 0)
@@ -482,9 +508,7 @@
             halo = jnp.where(low4, fewer, x)
         else:
             halo = jnp.where(low4, x, fewer)
-        low = edge[i, w_at, n, pl.ds(0, 4, stride=8), :]
-        high = edge[i, w_at, n, pl.ds(39, 4, stride=8), :]
-        return jnp.exp2(jnp.concatenate([low, high], axis=0) + halo)
+        return jnp.exp2(edge_sum[i, w_at, n] + halo)
 
     for n in range(4):
         def partner(v, dy):
@@ -509,13 +533,8 @@
                 total_w = total_w + (ahead + behind)
         rim_rows = total * (1.0 / SCALE) / total_w
 
-        lanes = slice(128 * n, 128 * n + 128)
-        top = shifted[4, n + 1, 8:136, :] + num[:, lanes]
-        ordered[n] = top * (1.0 / SCALE) / (1.0 + wsum[:, lanes])
-        pieces = [ordered[n, pl.ds(c, 16, stride=8), :] for c in range(8)]
-        pieces = [jnp.where(low4, rim_rows, pieces[0][0:8]), pieces[0][8:16]] + pieces[1:7] + [
-            pieces[7][0:8], jnp.where(low4, pieces[7][8:16], rim_rows)]
-        out_ref[4 * n:4 * n + 4] = jnp.concatenate(pieces, axis=0).T.reshape(4, 32, 128)
+        columns = jnp.concatenate([rim_rows, jnp.zeros((112, 128), F32), rim_rows], axis=0).T.reshape(4, 32, 128)
+        out_ref[4 * n:4 * n + 4] = jnp.where(is_rim, columns, out_ref[4 * n:4 * n + 4])
 
     for copy, dst, dz, dx, dy in plane_copies:
         pl.when(there(dz, dx, dy))(copy.wait_send)
@@ -546,7 +565,7 @@
             vmem(2, 384, 1024, dtype=BF16), vmem(2, 2, 4, 384, 128),
             vmem(128, 512), vmem(128, 512),
             vmem(208, 1024, dtype=BF16), vmem(2, 4, 208, 128),
-            vmem(13, 2, 4, 64, 128), vmem(9, 4, 3, 8, 128),
+            vmem(13, 2, 4, 64, 128), vmem(13, 2, 4, 8, 128), vmem(9, 4, 3, 8, 128),
             vmem(4, 128, 128),
             pltpu.SemaphoreType.DMA((2,)),
             pltpu.SemaphoreType.DMA((28,)),

time: 16.2 us -> 15.8 us (0.975)
  Pallas kernels: 15.4 us -> 14.9 us
    pallas_call x1, Pallas kernels: 15.4 us -> 14.9 us  [shards(): pl.pallas_call(kernel, out_shape=jax.ShapeDtypeStruct(noisy.shape, F32),...]
where the time goes in v4:
time: 15.8 us; the launch traced here: 15.6 us
  Pallas kernels  14.9 us (94%)
  local copies, waits for them, and re-layouts  0.71 us (4%)
    pallas_call x1, Pallas kernels, shards(): pl.pallas_call(kernel, out_shape=jax.ShapeDtypeStruct(noisy.shape, F32),...  14.9 us
    unnamed x1, local copies, waits for them, and re-layouts  0.71 us

profile of v4, /device:TPU:1, one launch (start us, length us, event | category | flops | bytes accessed | tf_op | source)
XLA Modules:
  0.0 15.6 jit_solution(4264524369440893726)
XLA Ops:
  0.0 14.9 %shard_map.28 = f32[16,32,128]{2,1,0:T(8,128)S(1)} custom-call(f32[16,32,128]{2,1,0:T(8,128)} %x_ref.1, bf16[5,2,640,256]{3,2,1,0:T(8,128)(2,1)} %constant.2.clone.box_hbm), custom_call_target="tpu_custom_call" | custom-call | tf_op jit(solution)/shard_map/pallas_call | solution.py:551
  14.9 0.7 %copy.4 = f32[16,32,128]{2,1,0:T(8,128)} copy(f32[16,32,128]{2,1,0:T(8,128)S(1)} %shard_map.28) | data formatting | bytes 524288

commit v5 on v4

--- a/solution.py
+++ b/solution.py
@@ -66,7 +66,7 @@
     around = [(dz, dx) for dz in (-1, 0, 1) for dx in (-1, 0, 1)]
     beside = [o for o in around if o != (0, 0)]
     barrier = pltpu.get_barrier_semaphore()
-    direct_to = nz - 2
+    direct_to = nz - 3
     for dy in (-1, 1):
         for dz, dx in around:
             greets = jnp.logical_and(even, there(dz, dx, dy))

time: 15.8 us -> 15.8 us (level)
  no operation moved by 1% of the time
where the time goes in v5:
time: 15.8 us; the launch traced here: 15.6 us
  Pallas kernels  14.9 us (94%)
  local copies, waits for them, and re-layouts  0.71 us (4%)
    pallas_call x1, Pallas kernels, shards(): pl.pallas_call(kernel, out_shape=jax.ShapeDtypeStruct(noisy.shape, F32),...  14.9 us
    unnamed x1, local copies, waits for them, and re-layouts  0.71 us

profile of v5, /device:TPU:1, one launch (start us, length us, event | category | flops | bytes accessed | tf_op | source)
XLA Modules:
  0.0 15.6 jit_solution(5429152749996359046)
XLA Ops:
  0.0 14.9 %shard_map.28 = f32[16,32,128]{2,1,0:T(8,128)S(1)} custom-call(f32[16,32,128]{2,1,0:T(8,128)} %x_ref.1, bf16[5,2,640,256]{3,2,1,0:T(8,128)(2,1)} %constant.2.clone.box_hbm), custom_call_target="tpu_custom_call" | custom-call | tf_op jit(solution)/shard_map/pallas_call | solution.py:551
  14.9 0.7 %copy.4 = f32[16,32,128]{2,1,0:T(8,128)} copy(f32[16,32,128]{2,1,0:T(8,128)S(1)} %shard_map.28) | data formatting | bytes 524288
